TPU v7x, 32 devices: a whole 2x2x4 slice. The times are simulated.
32 devices in a mesh: ia: 4 (over y, x), ja: 4 (over z), ka: 2 (over core).
Axes of the slice: x: 2, y: 2, z: 4, core: 2. Of those that a mesh axis runs over, the one named last changes fastest.
Arguments:
- inputs: bfloat16 [4, 1024, 4096], P('ia', 'ja', 'ka'), may hold values from -0.09375 to 0.09375
- attn_out: bfloat16 [4, 1024, 4096], P(None, 'ja', ('ia', 'ka')), may hold values from -0.09375 to 0.09375
- grad_out: bfloat16 [4, 1024, 4096], P('ia', 'ja', 'ka'), may hold values from -6 to 6
- grad_query: bfloat16 [4, 1024, 4096], P(None, 'ja', ('ia', 'ka')), may hold values from -6 to 6
- grad_key: bfloat16 [4, 1024, 4096], P(None, 'ja', ('ia', 'ka')), may hold values from -6 to 6
- grad_value: bfloat16 [4, 1024, 4096], P(None, 'ja', ('ia', 'ka')), may hold values from -6 to 6
- query_weight: bfloat16 [4096, 4096], P('ka', ('ia', 'ja')), may hold values from -0.09375 to 0.09375
- key_weight: bfloat16 [4096, 4096], P('ka', ('ia', 'ja')), may hold values from -0.09375 to 0.09375
- value_weight: bfloat16 [4096, 4096], P('ka', ('ia', 'ja')), may hold values from -0.09375 to 0.09375
Outputs:
- grad_inputs: bfloat16 [4, 1024, 4096], P('ia', 'ja', 'ka')
- query_weight_grad: float32 [4096, 4096], P('ka', ('ia', 'ja'))
- key_weight_grad: float32 [4096, 4096], P('ka', ('ia', 'ja'))
- value_weight_grad: float32 [4096, 4096], P('ka', ('ia', 'ja'))
- output_weight_grad: float32 [4096, 4096], P(('ia', 'ja'), 'ka')
All inputs are finite; a program needn't handle non-finite values.
Results may differ from a plain program's by a relative error of at most 0.015.
Values may be sent and summed in bfloat16 or wider, within the bound.
No kernel may reach another device: no remote copies, remote signals or barrier semaphores. Data moves between devices by JAX's collectives and lax.ppermute only.
A program may use at most 128 MiB of HBM per device.

v0:
```python
import jax
import jax.numpy as jnp
from jax import lax
from jax.sharding import PartitionSpec as P


def project(grads, weight_piece):
    return jnp.einsum("btf,df->btd", grads, weight_piece, preferred_element_type=jnp.float32)


def fold_weights(query_weight, key_weight, value_weight, folder, initial):
    return folder(
        initial,
        (
            lax.all_gather(query_weight, "ja", axis=1, tiled=True),
            lax.all_gather(key_weight, "ja", axis=1, tiled=True),
            lax.all_gather(value_weight, "ja", axis=1, tiled=True),
        ),
        jnp.int32(0),
    )


def local(
    inputs,
    attn_out,
    grad_out,
    grad_query,
    grad_key,
    grad_value,
    query_weight,
    key_weight,
    value_weight,
):
    rows_all, grad_rows = (
        lax.all_gather(inputs, "ia", axis=0, tiled=True),
        lax.all_gather(grad_out, "ia", axis=0, tiled=True),
    )
    attn_full, query_full, key_full, value_full = (
        lax.all_gather(attn_out, "ka", axis=2, tiled=True),
        lax.all_gather(grad_query, "ka", axis=2, tiled=True),
        lax.all_gather(grad_key, "ka", axis=2, tiled=True),
        lax.all_gather(grad_value, "ka", axis=2, tiled=True),
    )
    query_term = jnp.einsum("btd,btf->df", rows_all, query_full, preferred_element_type=jnp.float32)
    key_term = jnp.einsum("btd,btf->df", rows_all, key_full, preferred_element_type=jnp.float32)
    value_term = jnp.einsum("btd,btf->df", rows_all, value_full, preferred_element_type=jnp.float32)
    output_term = jnp.einsum(
        "btf,btd->fd", attn_full, grad_rows, preferred_element_type=jnp.float32
    )
    query_weight_grad, key_weight_grad, value_weight_grad, output_weight_grad = (
        lax.psum_scatter(
            query_term.astype(jnp.bfloat16), "ja", scatter_dimension=1, tiled=True
        ).astype(jnp.float32),
        lax.psum_scatter(
            key_term.astype(jnp.bfloat16), "ja", scatter_dimension=1, tiled=True
        ).astype(jnp.float32),
        lax.psum_scatter(
            value_term.astype(jnp.bfloat16), "ja", scatter_dimension=1, tiled=True
        ).astype(jnp.float32),
        lax.psum_scatter(
            output_term.astype(jnp.bfloat16), "ja", scatter_dimension=0, tiled=True
        ).astype(jnp.float32),
    )
    grads_all = (query_full, key_full, value_full)
    blank_sum = jnp.zeros(
        (query_full.shape[0], query_full.shape[1], query_weight.shape[0]), jnp.float32
    )

    def add_all(running, pieces, offset):
        for grads, piece_block in zip(grads_all, pieces):
            running = running + project(grads, piece_block)
        return running

    partial_term = fold_weights(query_weight, key_weight, value_weight, add_all, blank_sum)
    owned_sum = lax.psum_scatter(partial_term, "ia", scatter_dimension=0, tiled=True)
    grad_inputs = owned_sum.astype(jnp.bfloat16)
    return (grad_inputs, query_weight_grad, key_weight_grad, value_weight_grad, output_weight_grad)


def solution(mesh):
    return jax.shard_map(
        local,
        mesh=mesh,
        in_specs=(
            P("ia", "ja", "ka"),
            P(None, "ja", ("ia", "ka")),
            P("ia", "ja", "ka"),
            P(None, "ja", ("ia", "ka")),
            P(None, "ja", ("ia", "ka")),
            P(None, "ja", ("ia", "ka")),
            P("ka", ("ia", "ja")),
            P("ka", ("ia", "ja")),
            P("ka", ("ia", "ja")),
        ),
        out_specs=(
            P("ia", "ja", "ka"),
            P("ka", ("ia", "ja")),
            P("ka", ("ia", "ja")),
            P("ka", ("ia", "ja")),
            P(("ia", "ja"), "ka"),
        ),
        check_vma=False,
    )
```

profile of v0, /device:TPU:0, one launch (start us, length us, event | category | flops | bytes accessed | tf_op | source)
XLA Modules:
  0.0 831.2 jit_solution(17682194603686879372)
XLA Ops:
  7.2 0.7 all-gather.10.cloned.1.call-update
  8.0 0.7 all-gather.22.cloned.1.call-update
  8.7 0.7 all-gather.14.cloned.1.call-update
  10.0 1.3 copy.19
  12.0 0.7 all-gather.20.cloned.1.call-update
  12.7 0.7 all-gather.16.cloned.1.call-update
  14.2 8.6 %all-gather.10.cloned.1.call-done = bf16[4,256,1024]{2,1,0:T(8,128)(2,1)} async-done(((bf16[4,256,512]{2,1,0:T(8,128)(2,1)}), bf16[4,256,1024]{2,1,0:T(8,128)(2,1)}) %all-gather.10.cloned.1.call-update) | async-done | bytes 2097168 | tf_op jit(solution)/shard_map/all_gather | solution.py:40
  22.9 55.7 %all-gather.22.cloned.1.call-done = bf16[4,256,2048]{2,1,0:T(8,128)(2,1)} async-done(((bf16[1,256,2048]{2,1,0:T(8,128)(2,1)}), bf16[4,256,2048]{2,1,0:T(8,128)(2,1)}) %all-gather.22.cloned.1.call-update) | async-done | bytes 4194320 | tf_op jit(solution)/shard_map/all_gather | solution.py:35
  78.6 9.4 %bitcast_convert_fusion.3 = bf16[2048,1024]{1,0:T(8,128)(2,1)} fusion(bf16[4,256,2048]{2,1,0:T(8,128)(2,1)} %all-gather.22.cloned.1.call-done, bf16[4,256,1024]{2,1,0:T(8,128)(2,1)} %all-gather.10.cloned.1.call-done), kind=kOutput, calls=%fused_computation.3 | convolution fusion | flops 4297064448 | bytes 10485760 | tf_op jit(solution)/shard_map/btd,btf->df/dot_general | solution.py:44
  88.1 2.7 all-gather.14.cloned.1.call-done
  90.8 9.5 %bitcast_convert_fusion.2 = bf16[2048,1024]{1,0:T(8,128)(2,1)} fusion(bf16[4,256,2048]{2,1,0:T(8,128)(2,1)} %all-gather.22.cloned.1.call-done, bf16[4,256,1024]{2,1,0:T(8,128)(2,1)} %all-gather.14.cloned.1.call-done), kind=kOutput, calls=%fused_computation.2 | convolution fusion | flops 4297064448 | bytes 10485760 | tf_op jit(solution)/shard_map/btd,btf->df/dot_general | solution.py:45
  100.5 3.5 all-gather.18.cloned.1.call-done
  104.0 9.4 %bitcast_convert_fusion.1 = bf16[2048,1024]{1,0:T(8,128)(2,1)} fusion(bf16[4,256,2048]{2,1,0:T(8,128)(2,1)} %all-gather.22.cloned.1.call-done, bf16[4,256,1024]{2,1,0:T(8,128)(2,1)} %all-gather.18.cloned.1.call-done), kind=kOutput, calls=%fused_computation.1 | convolution fusion | flops 4297064448 | bytes 10485760 | tf_op jit(solution)/shard_map/btd,btf->df/dot_general | solution.py:46
  113.5 4.2 all-gather.24.cloned.1.call-done
  117.7 55.6 %all-gather.26.cloned.1.call-done = bf16[4,256,2048]{2,1,0:T(8,128)(2,1)} async-done(((bf16[1,256,2048]{2,1,0:T(8,128)(2,1)}), bf16[4,256,2048]{2,1,0:T(8,128)(2,1)}) %all-gather.26.cloned.1.call-update) | async-done | bytes 4194320 | tf_op jit(solution)/shard_map/all_gather | solution.py:36
  173.3 9.3 %bitcast_convert_fusion = bf16[1024,2048]{1,0:T(8,128)(2,1)} fusion(bf16[4,256,1024]{1,2,0:T(8,128)(2,1)} %all-gather.24.cloned.1.call-done, bf16[4,256,2048]{2,1,0:T(8,128)(2,1)} %all-gather.26.cloned.1.call-done), kind=kOutput, calls=%fused_computation | convolution fusion | flops 4297064448 | bytes 10485760 | tf_op jit(solution)/shard_map/btf,btd->fd/dot_general | solution.py:47
  182.9 72.6 %all-gather.20.cloned.1.call-done = bf16[2048,1024]{1,0:T(8,128)(2,1)} async-done(((bf16[2048,256]{1,0:T(8,128)(2,1)}), bf16[2048,1024]{1,0:T(8,128)(2,1)}) %all-gather.20.cloned.1.call-update) | async-done | bytes 4194320 | tf_op jit(solution)/shard_map/all_gather | solution.py:17
  255.5 9.0 %fusion = f32[4,256,2048]{2,1,0:T(8,128)} fusion(bf16[4,256,1024]{2,1,0:T(8,128)(2,1)S(1)} %copy-done.2, bf16[2048,1024]{1,0:T(8,128)(2,1)} %all-gather.20.cloned.1.call-done), kind=kOutput, calls=%fused_computation.5 | convolution fusion | flops 4294967296 | bytes 14680064 | tf_op jit(solution)/shard_map/btf,df->btd/dot_general | solution.py:8
  264.5 71.3 %all-gather.16.cloned.1.call-done = bf16[2048,1024]{1,0:T(8,128)(2,1)} async-done(((bf16[2048,256]{1,0:T(8,128)(2,1)}), bf16[2048,1024]{1,0:T(8,128)(2,1)}) %all-gather.16.cloned.1.call-update) | async-done | bytes 4194320 | tf_op jit(solution)/shard_map/all_gather | solution.py:16
  335.8 10.6 %fusion.2 = f32[4,256,2048]{2,1,0:T(8,128)} fusion(bf16[4,256,1024]{2,1,0:T(8,128)(2,1)} %all-gather.14.cloned.1.call-done, bf16[2048,1024]{1,0:T(8,128)(2,1)} %all-gather.16.cloned.1.call-done), kind=kOutput, calls=%fused_computation.7 | convolution fusion | flops 4294967296 | bytes 14680064 | tf_op jit(solution)/shard_map/btf,df->btd/dot_general | solution.py:8
  346.4 69.7 %all-gather.12.cloned.1.call-done = bf16[2048,1024]{1,0:T(8,128)(2,1)} async-done(((bf16[2048,256]{1,0:T(8,128)(2,1)}), bf16[2048,1024]{1,0:T(8,128)(2,1)}) %all-gather.12.cloned.1.call-update) | async-done | bytes 4194320 | tf_op jit(solution)/shard_map/all_gather | solution.py:15
  416.2 12.2 %add_add_fusion = f32[4,256,2048]{2,1,0:T(8,128)} fusion(f32[4,256,2048]{2,1,0:T(8,128)} %fusion, f32[4,256,2048]{2,1,0:T(8,128)} %fusion.2, bf16[4,256,1024]{2,1,0:T(8,128)(2,1)S(1)} %copy-done.1, bf16[2048,1024]{1,0:T(8,128)(2,1)} %all-gather.12.cloned.1.call-done), kind=kOutput, calls=%fused_computation.4 | convolution fusion | flops 4299161600 | bytes 31457280 | tf_op jit(solution)/shard_map/btf,df->btd/dot_general | solution.py:8
  428.4 64.9 %reduce-scatter.8.cloned.1.call-done = bf16[2048,256]{1,0:T(8,128)(2,1)} async-done(((bf16[2048,1024]{1,0:T(8,128)(2,1)}), bf16[2048,256]{1,0:T(8,128)(2,1)}) %reduce-scatter.8.cloned.1.call-update) | async-done | bytes 1048592 | tf_op jit(solution)/shard_map/reduce_scatter | solution.py:51
  493.3 2.7 convert_element_type.29
  496.0 77.0 %reduce-scatter.10.cloned.1.call-done = bf16[2048,256]{1,0:T(8,128)(2,1)} async-done(((bf16[2048,1024]{1,0:T(8,128)(2,1)}), bf16[2048,256]{1,0:T(8,128)(2,1)}) %reduce-scatter.10.cloned.1.call-update) | async-done | bytes 1048592 | tf_op jit(solution)/shard_map/reduce_scatter | solution.py:54
  573.0 2.7 convert_element_type.31
  575.7 76.7 %reduce-scatter.12.cloned.1.call-done = bf16[2048,256]{1,0:T(8,128)(2,1)} async-done(((bf16[2048,1024]{1,0:T(8,128)(2,1)}), bf16[2048,256]{1,0:T(8,128)(2,1)}) %reduce-scatter.12.cloned.1.call-update) | async-done | bytes 1048592 | tf_op jit(solution)/shard_map/reduce_scatter | solution.py:57
  652.4 2.7 convert_element_type.33
  655.1 77.0 %reduce-scatter.14.cloned.1.call-done = bf16[256,2048]{1,0:T(8,128)(2,1)} async-done(((bf16[1024,2048]{1,0:T(8,128)(2,1)}), bf16[256,2048]{1,0:T(8,128)(2,1)}) %reduce-scatter.14.cloned.1.call-update) | async-done | bytes 1048592 | tf_op jit(solution)/shard_map/reduce_scatter | solution.py:60
  732.1 2.8 convert_element_type.35
  734.9 87.1 %reduce-scatter.16.cloned.1.call-done = f32[1,256,2048]{2,1,0:T(8,128)} async-done(((f32[4,256,2048]{2,1,0:T(8,128)}), f32[1,256,2048]{2,1,0:T(8,128)}) %reduce-scatter.16.cloned.1.call-update) | async-done | bytes 2097168
  822.0 2.7 convert_element_type.27
  (29 shorter events, 2.8 us)
Async XLA Ops:
  7.2 2.9 copy-start
  7.2 15.7 %all-gather.10.cloned.1.call-start = ((), (), s32[]{:S(2)}) async-start(), calls=%async_computation.5 | async-start | bytes 3145728 | tf_op jit(solution)/shard_map/all_gather | solution.py:40
  7.9 70.7 %all-gather.22.cloned.1.call-start = ((), (), s32[]{:S(2)}) async-start(), calls=%async_computation.11 | async-start | bytes 5242880 | tf_op jit(solution)/shard_map/all_gather | solution.py:35
  8.7 82.1 %all-gather.14.cloned.1.call-start = ((), (), s32[]{:S(2)}) async-start(), calls=%async_computation.7 | async-start | bytes 3145728 | tf_op jit(solution)/shard_map/all_gather | solution.py:41
  9.4 94.6 %all-gather.18.cloned.1.call-start = ((), (), s32[]{:S(2)}) async-start(), calls=%async_computation.9 | async-start | bytes 3145728 | tf_op jit(solution)/shard_map/all_gather | solution.py:42
  10.0 107.7 %all-gather.24.cloned.1.call-start = ((), (), s32[]{:S(2)}) async-start(), calls=%async_computation.15 | async-start | bytes 3145728 | tf_op jit(solution)/shard_map/all_gather | solution.py:39
  11.4 162.0 %all-gather.26.cloned.1.call-start = ((), (), s32[]{:S(2)}) async-start(), calls=%async_computation.16 | async-start | bytes 5242880 | tf_op jit(solution)/shard_map/all_gather | solution.py:36
  11.9 243.5 %all-gather.20.cloned.1.call-start = ((), (), s32[]{:S(2)}) async-start(), calls=%async_computation.10 | async-start | bytes 5242880 | tf_op jit(solution)/shard_map/all_gather | solution.py:17
  12.7 323.1 %all-gather.16.cloned.1.call-start = ((), (), s32[]{:S(2)}) async-start(), calls=%async_computation.8 | async-start | bytes 5242880 | tf_op jit(solution)/shard_map/all_gather | solution.py:16
  13.4 402.7 %all-gather.12.cloned.1.call-start = ((), (), s32[]{:S(2)}) async-start(), calls=%async_computation.6 | async-start | bytes 5242880 | tf_op jit(solution)/shard_map/all_gather | solution.py:15
  14.2 479.1 %reduce-scatter.8.cloned.1.call-start = ((), (), s32[]{:S(2)}) async-start(), calls=%async_computation.12 | async-start | bytes 5242880 | tf_op jit(solution)/shard_map/reduce_scatter | solution.py:51
  88.0 485.0 %reduce-scatter.10.cloned.1.call-start = ((), (), s32[]{:S(2)}) async-start(), calls=%async_computation.13 | async-start | bytes 5242880 | tf_op jit(solution)/shard_map/reduce_scatter | solution.py:54
  100.3 552.2 %reduce-scatter.12.cloned.1.call-start = ((), (), s32[]{:S(2)}) async-start(), calls=%async_computation.14 | async-start | bytes 5242880 | tf_op jit(solution)/shard_map/reduce_scatter | solution.py:57
  113.4 618.7 %reduce-scatter.14.cloned.1.call-start = ((), (), s32[]{:S(2)}) async-start(), calls=%async_computation.17 | async-start | bytes 5242880 | tf_op jit(solution)/shard_map/reduce_scatter | solution.py:60
  182.6 72.9 %copy-start.2 = (bf16[4,256,1024]{2,1,0:T(8,128)(2,1)S(1)}, bf16[4,256,1024]{2,1,0:T(8,128)(2,1)}, u32[]{:S(2)}) copy-start(bf16[4,256,1024]{2,1,0:T(8,128)(2,1)} %all-gather.18.cloned.1.call-done) | copy-start | bytes 6291460
  182.6 639.4 %reduce-scatter.16.cloned.1.call-start = ((), (), s32[]{:S(2)}) async-start(), calls=%async_computation.18 | async-start | bytes 10485760
  264.5 151.7 %copy-start.1 = (bf16[4,256,1024]{2,1,0:T(8,128)(2,1)S(1)}, bf16[4,256,1024]{2,1,0:T(8,128)(2,1)}, u32[]{:S(2)}) copy-start(bf16[4,256,1024]{2,1,0:T(8,128)(2,1)} %all-gather.10.cloned.1.call-done) | copy-start | bytes 6291460
Sparse Core Ops, SparseCore 0:
  9.6 13.2 all-gather.9
  24.7 53.8 all-gather.21
  80.2 10.5 all-gather.13
  92.2 11.7 all-gather.17
  105.9 11.7 all-gather.23
  119.4 53.8 all-gather.25
  174.9 80.5 all-gather.19
  257.0 78.7 all-gather.15
  337.4 78.7 all-gather.11
  418.3 74.9 reduce-scatter.7
  495.7 77.2 reduce-scatter.9
  575.1 77.2 reduce-scatter.11
  654.8 77.2 reduce-scatter.13
  735.1 86.8 reduce-scatter.15
where the time goes:
time: 832 us; the launch traced here: 831 us
  waiting for transfers between devices  732 us (88%)
  matrix products  69.4 us (8%)
  between operations  14 us (2%)
  other arithmetic  13.6 us (2%)
    unnamed x15, waiting for transfers between devices  92.3 us
    reduce_scatter x1, waiting for transfers between devices, local(): lax.psum_scatter(output_term.astype(jnp.bfloat16), 'ja', scatter_dimensio...  77 us
    reduce_scatter x1, waiting for transfers between devices, local(): lax.psum_scatter(key_term.astype(jnp.bfloat16), 'ja', scatter_dimension=1...  77 us
    reduce_scatter x1, waiting for transfers between devices, local(): lax.psum_scatter(value_term.astype(jnp.bfloat16), 'ja', scatter_dimension...  76.7 us
    all_gather x1, waiting for transfers between devices, fold_weights(): lax.all_gather(value_weight, 'ja', axis=1, tiled=True)  72.6 us
    all_gather x1, waiting for transfers between devices, fold_weights(): lax.all_gather(key_weight, 'ja', axis=1, tiled=True)  71.3 us
    all_gather x1, waiting for transfers between devices, fold_weights(): lax.all_gather(query_weight, 'ja', axis=1, tiled=True)  69.7 us
    reduce_scatter x1, waiting for transfers between devices, local(): lax.psum_scatter(query_term.astype(jnp.bfloat16), 'ja', scatter_dimension...  64.9 us
  transfers between devices with their start and end apart: 14, of which 14 were waited for; matrix products, arithmetic and copies ran while one was open for 10% of the time, Pallas kernels for 0%

commit v1 on v0

v1 whole, which is shorter than its diff:
```python
import jax
import jax.numpy as jnp
from jax import lax
from jax.sharding import PartitionSpec as P

BF16 = jnp.bfloat16
F32 = jnp.float32


def ring_place(j, n):
    return jnp.where(j % 2 == 1, (j + 1) // 2, (n - j // 2) % n)


def ring_pairs(n):
    order = [0] + list(range(1, n, 2)) + list(range(n - 2, 0, -2))
    return [(order[p], order[(p + 1) % n]) for p in range(n)]


def dot_rows(a, b):
    return lax.dot_general(a, b, (((0,), (0,)), ((), ())), preferred_element_type=F32)


def dot_cols(a, b):
    return lax.dot_general(a, b, (((1,), (1,)), ((), ())), preferred_element_type=F32)


def build(mesh):
    ni, nj, nk = mesh.shape["ia"], mesh.shape["ja"], mesh.shape["ka"]
    assert ni == 4 and nj % nk == 0
    per = nj // nk
    swap_x = [(i, i ^ 1) for i in range(ni)]
    swap_y = [(i, i ^ 2) for i in range(ni)]
    ring = ring_pairs(nj)
    core_ring = [(k, (k + 1) % nk) for k in range(nk)]

    def deal_pairs(step, dy):
        pairs = []
        for i in range(ni):
            for j in range(nj):
                for k in range(nk):
                    to_j, to_k = per * k + (j + step) % per, j // per
                    pairs.append(
                        ((i * nj + j) * nk + k, ((i ^ (2 * dy)) * nj + to_j) * nk + to_k)
                    )
        return pairs

    def local(
        inputs,
        attn_out,
        grad_out,
        grad_query,
        grad_key,
        grad_value,
        query_weight,
        key_weight,
        value_weight,
    ):
        i, j, k = lax.axis_index("ia"), lax.axis_index("ja"), lax.axis_index("ka")
        tok, width = inputs.shape[1], inputs.shape[2]
        feat = grad_query.shape[2] // per
        place = ring_place(j, nj)
        grads = (grad_query, grad_key, grad_value)

        rows = inputs.reshape(tok, width)
        blocks = []
        for step in range(nj):
            blocks.append(rows)
            blocks.append(lax.ppermute(rows, "ia", swap_x))
            if step < nj - 1:
                rows = lax.ppermute(rows, "ja", ring)
        x_all = jnp.concatenate(blocks, axis=0)

        w_own = jnp.concatenate((query_weight, key_weight, value_weight), axis=1)
        w_both = jnp.concatenate((w_own, lax.ppermute(w_own, "ia", swap_y)), axis=1)

        go_own = grad_out.reshape(tok, width)
        go_pair = jnp.concatenate((go_own, lax.ppermute(go_own, "ia", swap_x)), axis=0)
        go_all = jnp.concatenate((go_pair, lax.ppermute(go_pair, "ia", swap_y)), axis=0)

        attn = jnp.concatenate(
            [lax.dynamic_index_in_dim(attn_out, i ^ r, 0, keepdims=False) for r in range(ni)], axis=0
        )
        attn_list = [attn]
        for _ in range(nk - 1):
            attn_list.append(lax.ppermute(attn_list[-1], "ka", core_ring))
        attn_all = jnp.stack(attn_list)

        g_all = jnp.zeros((nj, 2 * tok, 6 * feat), BF16)
        for dy in range(2):
            for step in range(per):
                chunk = (j + step) % per
                piece = jnp.concatenate(
                    [
                        jnp.concatenate(
                            [
                                lax.dynamic_slice(
                                    grad, (i ^ (2 * dy) ^ dx, 0, chunk * feat), (1, tok, feat)
                                ).reshape(tok, feat)
                                for grad in grads
                            ],
                            axis=1,
                        )
                        for dx in range(2)
                    ],
                    axis=0,
                )
                piece = lax.ppermute(piece, ("ia", "ja", "ka"), deal_pairs(step, dy))
                for hop in range(nk):
                    source = per * ((k - hop) % nk) + (j % per - step) % per
                    slot = (place - ring_place(source, nj)) % nj
                    g_all = lax.dynamic_update_slice(
                        g_all, piece[None], (slot, 0, dy * 3 * feat)
                    )
                    if hop < nk - 1:
                        piece = lax.ppermute(piece, "ka", core_ring)

        def output_chunk(step):
            back = (place - step) % nj
            dest = jnp.where(
                back == 0, 0, jnp.where(back <= nj // 2, 2 * back - 1, 2 * (nj - back))
            )
            part = lax.dynamic_slice(
                attn_all, ((k - dest // per) % nk, 0, (dest % per) * feat), (1, ni * tok, feat)
            )
            return dot_rows(part.reshape(ni * tok, feat), go_all)

        moving = output_chunk(1).astype(BF16)
        for step in range(1, nj):
            moving = lax.ppermute(moving, "ja", ring)
            total = output_chunk((step + 1) % nj) + moving.astype(F32)
            moving = total.astype(BF16)
        output_weight_grad = total

        def input_chunk(step):
            other = dot_cols(g_all[step % nj, tok:], w_both).astype(BF16)
            other = lax.ppermute(other, "ia", swap_x)
            return dot_cols(g_all[step % nj, :tok], w_both) + other.astype(F32)

        moving = input_chunk(1).astype(BF16)
        for step in range(1, nj):
            moving = lax.ppermute(moving, "ja", ring)
            moving = (input_chunk(step + 1) + moving.astype(F32)).astype(BF16)
        grad_inputs = moving.reshape(inputs.shape)

        g_flat = g_all.reshape(nj * 2 * tok, 6 * feat)
        weight_grads = []
        for w in range(3):
            other = dot_rows(x_all, g_flat[:, (3 + w) * feat : (4 + w) * feat]).astype(BF16)
            other = lax.ppermute(other, "ia", swap_y)
            weight_grads.append(
                dot_rows(x_all, g_flat[:, w * feat : (w + 1) * feat]) + other.astype(F32)
            )
        return (grad_inputs, *weight_grads, output_weight_grad)

    return local


def solution(mesh):
    return jax.shard_map(
        build(mesh),
        mesh=mesh,
        in_specs=(
            P("ia", "ja", "ka"),
            P(None, "ja", ("ia", "ka")),
            P("ia", "ja", "ka"),
            P(None, "ja", ("ia", "ka")),
            P(None, "ja", ("ia", "ka")),
            P(None, "ja", ("ia", "ka")),
            P("ka", ("ia", "ja")),
            P("ka", ("ia", "ja")),
            P("ka", ("ia", "ja")),
        ),
        out_specs=(
            P("ia", "ja", "ka"),
            P("ka", ("ia", "ja")),
            P("ka", ("ia", "ja")),
            P("ka", ("ia", "ja")),
            P(("ia", "ja"), "ka"),
        ),
        check_vma=False,
    )
```

time: 832 us -> 394 us (0.47)
  waiting for transfers between devices: 732 us -> 203 us
  starting transfers between devices: 0.95 us -> 81.1 us
  local copies, waits for them, and re-layouts: 1.32 us -> 23.5 us
  between operations: 14 us -> 1.41 us
    all_gather x9 -> x0, waiting for transfers between devices: 344 us -> none  [the longest x1 72.6 us: fold_weights(): lax.all_gather(value_weight, 'ja', axis=1, tiled=True)]
    reduce_scatter x4 -> x0, waiting for transfers between devices: 296 us -> none  [the longest x1 77 us: local(): lax.psum_scatter(output_term.astype(jnp.bfloat16), 'ja', scatter_dimensio...]
    ppermute x0 -> x32, waiting for transfers between devices: none -> 203 us  [the longest x1 74.3 us: local(): lax.ppermute(go_pair, 'ia', swap_y)]
    unnamed x15 -> x0, waiting for transfers between devices: 92.3 us -> none
    ppermute x0 -> x32, starting transfers between devices: none -> 81.1 us  [the longest x4 36.3 us: local(): piece = lax.ppermute(piece, 'ka', core_ring)]
    convert_element_type x5 -> x0, other arithmetic: 13.6 us -> none  [the longest x4 10.9 us: local(): query_weight_grad, key_weight_grad, value_weight_grad, output_weight_grad...]
    concatenate x0 -> x7, other arithmetic: none -> 12.2 us  [the longest x4 6.12 us: local(): jnp.concatenate([jnp.concatenate([lax.dynamic_slice(grad, (i ^ 2 * dy ^ d...]
    unnamed x7 -> x32, local copies, waits for them, and re-layouts: 1.32 us -> 12.5 us
  transfers between devices with their start and end apart: 14 -> 32, of which waited for: 14 -> 12; matrix products, arithmetic and copies ran while one was open for 10% -> 25% of each run, Pallas kernels for 0% -> 0%
where the time goes in v1:
time: 394 us; the launch traced here: 388 us
  waiting for transfers between devices  203 us (52%)
  starting transfers between devices  81.1 us (21%)
  matrix products  66.3 us (17%)
  local copies, waits for them, and re-layouts  23.5 us (6%)
  other arithmetic  12.2 us (3%)
    ppermute x1, waiting for transfers between devices, local(): lax.ppermute(go_pair, 'ia', swap_y)  74.3 us
    ppermute x6, waiting for transfers between devices, local(): moving = lax.ppermute(moving, 'ja', ring)  62.5 us
    dot_general x10, matrix products, dot_rows(): lax.dot_general(a, b, (((0,), (0,)), ((), ())), preferred_element_type=F32)  42.6 us
    ppermute x4, starting transfers between devices, local(): piece = lax.ppermute(piece, 'ka', core_ring)  36.3 us
    ppermute x3, waiting for transfers between devices, local(): rows = lax.ppermute(rows, 'ja', ring)  25.8 us
    dot_general x8, matrix products, dot_cols(): lax.dot_general(a, b, (((1,), (1,)), ((), ())), preferred_element_type=F32)  23.6 us
    ppermute x4, starting transfers between devices, local(): piece = lax.ppermute(piece, ('ia', 'ja', 'ka'), deal_pairs(step, dy))  14.6 us
    unnamed x32, local copies, waits for them, and re-layouts  12.5 us
  transfers between devices with their start and end apart: 32, of which 12 were waited for; matrix products, arithmetic and copies ran while one was open for 25% of the time, Pallas kernels for 0%

profile of v1, /device:TPU:0, one launch (start us, length us, event | category | flops | bytes accessed | tf_op | source)
XLA Modules:
  0.0 387.6 jit_solution(13899673228808551083)
XLA Ops:
  0.6 3.0 collective-permute-start.16
  10.8 7.4 %collective-permute-start = (bf16[512,768]{1,0:T(8,128)(2,1)}, bf16[512,768]{1,0:T(8,128)(2,1)}, u32[]{:S(2)}, u32[]{:S(2)}) collective-permute-start(bf16[512,768]{1,0:T(8,128)(2,1)} %maximum_maximum_fusion), channel_id=1, source_target_pairs={{0,0},{1,4},{2,2},{3,6},{4,1},{5,5},{6,3},{7,7},{8,8},{9,12},{10,1... | collective-permute-start | bytes 2359304 | tf_op jit(solution)/shard_map/ppermute | solution.py:107
  40.5 5.8 %collective-permute-done.2 = bf16[512,768]{1,0:T(8,128)(2,1)} collective-permute-done((bf16[512,768]{1,0:T(8,128)(2,1)}, bf16[512,768]{1,0:T(8,128)(2,1)}, u32[]{:S(2)}, u32[]{:S(2)}) %collective-permute-start.2) | collective-permute-done | bytes 786464 | tf_op jit(solution)/shard_map/ppermute | solution.py:107
  46.3 3.1 collective-permute-start.6
  49.6 13.9 %collective-permute-start.1 = (bf16[512,768]{1,0:T(8,128)(2,1)}, bf16[512,768]{1,0:T(8,128)(2,1)S(1)}, u32[]{:S(2)}, u32[]{:S(2)}) collective-permute-start(bf16[512,768]{1,0:T(8,128)(2,1)} %collective-permute-done), channel_id=1, source_target_pairs={{0,1},{1,0},{2,3},{3,2},{4,5},{5,4},{6,7},{7,6},{8,9},{9,8},{10,11... | collective-permute-start | bytes 2359304 | tf_op jit(solution)/shard_map/ppermute | solution.py:115
  66.9 22.2 %collective-permute-start.3 = (bf16[512,768]{1,0:T(8,128)(2,1)}, bf16[512,768]{1,0:T(8,128)(2,1)S(1)}, u32[]{:S(2)}, u32[]{:S(2)}) collective-permute-start(bf16[512,768]{1,0:T(8,128)(2,1)} %collective-permute-done.2), channel_id=1, source_target_pairs={{0,1},{1,0},{2,3},{3,2},{4,5},{5,4},{6,7},{7,6},{8,9},{9,8},{10,11... | collective-permute-start | bytes 2359304 | tf_op jit(solution)/shard_map/ppermute | solution.py:115
  98.7 6.0 %collective-permute-start.19 = (bf16[256,2048]{1,0:T(8,128)(2,1)}, bf16[256,2048]{1,0:T(8,128)(2,1)S(1)}, u32[]{:S(2)}, u32[]{:S(2)}) collective-permute-start(bf16[256,2048]{1,0:T(8,128)(2,1)} %collective-permute-done.17), channel_id=1, source_target_pairs={{0,2},{2,6},{6,4},{4,0},{1,3},{3,7},{7,5},{5,1},{8,10},{10,14},{14... | collective-permute-start | bytes 3145736 | tf_op jit(solution)/shard_map/ppermute | solution.py:70
  105.0 25.8 %collective-permute-done.19 = bf16[256,2048]{1,0:T(8,128)(2,1)S(1)} collective-permute-done((bf16[256,2048]{1,0:T(8,128)(2,1)}, bf16[256,2048]{1,0:T(8,128)(2,1)S(1)}, u32[]{:S(2)}, u32[]{:S(2)}) %collective-permute-start.19) | collective-permute-done | bytes 1048608 | tf_op jit(solution)/shard_map/ppermute | solution.py:70
  132.7 74.3 %collective-permute-done.28 = bf16[512,2048]{1,0:T(8,128)(2,1)S(1)} collective-permute-done((bf16[512,2048]{1,0:T(8,128)(2,1)S(1)}, bf16[512,2048]{1,0:T(8,128)(2,1)S(1)}, u32[]{:S(2)}, u32[]{:S(2)}) %collective-permute-start.28) | collective-permute-done | bytes 2097184 | tf_op jit(solution)/shard_map/ppermute | solution.py:78
  207.0 4.0 %convolution_convert_fusion = bf16[256,2048]{1,0:T(8,128)(2,1)} fusion(s32[]{:T(128)S(6)} %select_n.473, s32[]{:T(128)S(6)} %select_n.475, bf16[1,1024,512]{2,1,0:T(8,128)(2,1)S(1)} %copy-done.4, bf16[1,1024,512]{2,1,0:T(8,128)(2,1)S(1)} %bitcast.141, bf16[512,2048]{1,0:T(8,128)(2,1)S(1)} %collective-permute-done.28, ...), kind=kOutput, calls=%fused_computation.29 | convolution fusion | flops 1087897600 | bytes 7340040 | tf_op jit(solution)/shard_map/dot_general | solution.py:20
  216.1 2.8 convolution_convert_fusion.2
  226.1 11.0 %collective-permute-done.22 = bf16[256,2048]{1,0:T(8,128)(2,1)S(1)} collective-permute-done((bf16[256,2048]{1,0:T(8,128)(2,1)S(1)}, bf16[256,2048]{1,0:T(8,128)(2,1)S(1)}, u32[]{:S(2)}, u32[]{:S(2)}) %collective-permute-start.22) | collective-permute-done | bytes 1048608 | tf_op jit(solution)/shard_map/ppermute | solution.py:68
  237.7 3.6 convolution_convert_fusion.7
  241.4 3.6 convolution_convert_fusion.6
  245.0 2.9 convolution_convert_fusion.5
  247.9 11.7 %collective-permute-done.12 = bf16[256,2048]{1,0:T(8,128)(2,1)} collective-permute-done((bf16[256,2048]{1,0:T(8,128)(2,1)}, bf16[256,2048]{1,0:T(8,128)(2,1)}, u32[]{:S(2)}, u32[]{:S(2)}) %collective-permute-start.12) | collective-permute-done | bytes 1048608 | tf_op jit(solution)/shard_map/ppermute | solution.py:136
  259.7 4.0 %fusion.6 = bf16[256,2048]{1,0:T(8,128)(2,1)} fusion(bf16[2048,1536]{1,0:T(8,128)(2,1)S(1)} %constant_dynamic-update-slice_fusion, bf16[256,2048]{1,0:T(8,128)(2,1)} %collective-permute-done.12, bf16[4,512,1536]{2,1,0:T(8,128)(2,1)S(1)} %bitcast_dynamic-update-slice_fusion), kind=kOutput, calls=%fused_computation.26 | convolution fusion | flops 1612185600 | bytes 9175040 | tf_op jit(solution)/shard_map/dot_general | solution.py:24
  263.7 5.0 %collective-permute-start.13 = (bf16[256,2048]{1,0:T(8,128)(2,1)}, bf16[256,2048]{1,0:T(8,128)(2,1)S(1)}, u32[]{:S(2)}, u32[]{:S(2)}) collective-permute-start(bf16[256,2048]{1,0:T(8,128)(2,1)} %fusion.6), channel_id=1, source_target_pairs={{0,2},{2,6},{6,4},{4,0},{1,3},{3,7},{7,5},{5,1},{8,10},{10,14},{14... | collective-permute-start | bytes 3145736 | tf_op jit(solution)/shard_map/ppermute | solution.py:141
  268.7 4.2 %fusion.8 = bf16[256,2048]{1,0:T(8,128)(2,1)} fusion(bf16[256,2048]{1,0:T(8,128)(2,1)} %collective-permute-done.29, s32[]{:T(128)S(6)} %select_n.465, s32[]{:T(128)S(6)} %select_n.467, bf16[1,1024,512]{2,1,0:T(8,128)(2,1)S(1)} %copy-done.4, bf16[1,1024,512]{2,1,0:T(8,128)(2,1)S(1)} %bitcast.142, bf16[512,2048]{1,0:T(8,128)(2,1)S(1)} %collective-permute-done.28, ...), kind=kOutput, calls=%fused_computation.28 | convolution fusion | flops 1088946176 | bytes 8388616 | tf_op jit(solution)/shard_map/dot_general | solution.py:20
  272.8 11.7 %collective-permute-done.23 = bf16[2048,256]{1,0:T(8,128)(2,1)} collective-permute-done((bf16[2048,256]{1,0:T(8,128)(2,1)}, bf16[2048,256]{1,0:T(8,128)(2,1)}, u32[]{:S(2)}, u32[]{:S(2)}) %collective-permute-start.23) | collective-permute-done | bytes 1048608 | tf_op jit(solution)/shard_map/ppermute | solution.py:149
  286.1 5.2 %convolution_add_fusion.5 = f32[2048,256]{1,0:T(8,128)} fusion(bf16[2048,2048]{1,0:T(8,128)(2,1)S(1)} %constant_dynamic-update-slice_fusion.4, bf16[2048,256]{1,0:T(8,128)(2,1)} %collective-permute-done.23, bf16[2048,1536]{1,0:T(8,128)(2,1)S(1)} %bitcast.134), kind=kOutput, calls=%fused_computation.15 | convolution fusion | flops 2148532224 | bytes 12582912 | tf_op jit(solution)/shard_map/dot_general | solution.py:20
  297.1 4.4 %fusion.5 = bf16[256,2048]{1,0:T(8,128)(2,1)} fusion(bf16[2048,1536]{1,0:T(8,128)(2,1)S(1)} %constant_dynamic-update-slice_fusion, bf16[256,2048]{1,0:T(8,128)(2,1)} %copy-done.8, bf16[256,2048]{1,0:T(8,128)(2,1)} %copy-done.7, bf16[4,512,1536]{2,1,0:T(8,128)(2,1)S(1)} %bitcast_dynamic-update-slice_fusion), kind=kOutput, calls=%fused_computation.25 | convolution fusion | flops 1613234176 | bytes 10223616 | tf_op jit(solution)/shard_map/dot_general | solution.py:24
  301.5 13.6 %collective-permute-done.30 = bf16[256,2048]{1,0:T(8,128)(2,1)} collective-permute-done((bf16[256,2048]{1,0:T(8,128)(2,1)}, bf16[256,2048]{1,0:T(8,128)(2,1)}, u32[]{:S(2)}, u32[]{:S(2)}) %collective-permute-start.30) | collective-permute-done | bytes 1048608 | tf_op jit(solution)/shard_map/ppermute | solution.py:129
  315.1 4.1 %fusion.7 = bf16[256,2048]{1,0:T(8,128)(2,1)} fusion(bf16[256,2048]{1,0:T(8,128)(2,1)} %collective-permute-done.30, s32[]{:T(128)S(6)} %select_n.457, s32[]{:T(128)S(6)} %select_n.459, bf16[1,1024,512]{2,1,0:T(8,128)(2,1)S(1)} %copy-done.4, bf16[1,1024,512]{2,1,0:T(8,128)(2,1)S(1)} %bitcast.143, bf16[512,2048]{1,0:T(8,128)(2,1)S(1)} %collective-permute-done.28, ...), kind=kOutput, calls=%fused_computation.27 | convolution fusion | flops 1088946176 | bytes 8388616 | tf_op jit(solution)/shard_map/dot_general | solution.py:20
  319.5 5.2 %convolution_add_fusion.4 = f32[2048,256]{1,0:T(8,128)} fusion(bf16[2048,2048]{1,0:T(8,128)(2,1)S(1)} %constant_dynamic-update-slice_fusion.4, bf16[2048,256]{1,0:T(8,128)(2,1)} %collective-permute-done.24, bf16[2048,1536]{1,0:T(8,128)(2,1)S(1)} %bitcast.135), kind=kOutput, calls=%fused_computation.14 | convolution fusion | flops 2148532224 | bytes 12582912 | tf_op jit(solution)/shard_map/dot_general | solution.py:20
  324.8 17.7 %collective-permute-done.14 = bf16[256,2048]{1,0:T(8,128)(2,1)} collective-permute-done((bf16[256,2048]{1,0:T(8,128)(2,1)}, bf16[256,2048]{1,0:T(8,128)(2,1)}, u32[]{:S(2)}, u32[]{:S(2)}) %collective-permute-start.14) | collective-permute-done | bytes 1048608 | tf_op jit(solution)/shard_map/ppermute | solution.py:141
  342.4 3.1 fusion.4
  345.6 5.2 %convolution_add_fusion.3 = f32[2048,256]{1,0:T(8,128)} fusion(bf16[2048,2048]{1,0:T(8,128)(2,1)S(1)} %constant_dynamic-update-slice_fusion.4, bf16[2048,256]{1,0:T(8,128)(2,1)} %collective-permute-done.25, bf16[2048,1536]{1,0:T(8,128)(2,1)S(1)} %bitcast.136), kind=kOutput, calls=%fused_computation.13 | convolution fusion | flops 2148532224 | bytes 12582912 | tf_op jit(solution)/shard_map/dot_general | solution.py:20
  350.9 14.0 %collective-permute-done.31 = bf16[256,2048]{1,0:T(8,128)(2,1)} collective-permute-done((bf16[256,2048]{1,0:T(8,128)(2,1)}, bf16[256,2048]{1,0:T(8,128)(2,1)}, u32[]{:S(2)}, u32[]{:S(2)}) %collective-permute-start.31) | collective-permute-done | bytes 1048608 | tf_op jit(solution)/shard_map/ppermute | solution.py:129
  364.9 4.5 %convolution_add_fusion.2 = f32[256,2048]{1,0:T(8,128)} fusion(bf16[256,2048]{1,0:T(8,128)(2,1)} %collective-permute-done.31, s32[]{:T(128)S(6)} %select_n.449, s32[]{:T(128)S(6)} %select_n.451, bf16[1,1024,512]{2,1,0:T(8,128)(2,1)S(1)} %copy-done.4, bf16[1,1024,512]{2,1,0:T(8,128)(2,1)S(1)} %bitcast.144, ...), kind=kOutput, calls=%fused_computation.12 | convolution fusion | flops 1088421888 | bytes 9437192 | tf_op jit(solution)/shard_map/dot_general | solution.py:20
  369.4 14.9 %collective-permute-done.15 = bf16[256,2048]{1,0:T(8,128)(2,1)S(1)} collective-permute-done((bf16[256,2048]{1,0:T(8,128)(2,1)S(1)}, bf16[256,2048]{1,0:T(8,128)(2,1)S(1)}, u32[]{:S(2)}, u32[]{:S(2)}) %collective-permute-start.15) | collective-permute-done | bytes 1048608 | tf_op jit(solution)/shard_map/ppermute | solution.py:141
  384.3 2.8 fusion.9
  (104 shorter events, 65.1 us)
Async XLA Ops:
  0.6 88.6 %collective-permute-start.16 = (bf16[256,2048]{1,0:T(8,128)(2,1)}, bf16[256,2048]{1,0:T(8,128)(2,1)}, u32[]{:S(2)}, u32[]{:S(2)}) collective-permute-start(bf16[256,2048]{1,0:T(8,128)(2,1)} %bitcast.137), channel_id=1, source_target_pairs={{0,8},{8,0},{16,24},{24,16},{1,9},{9,1},{17,25},{25,17},{2,10},{10... | collective-permute-start | bytes 3145736 | tf_op jit(solution)/shard_map/ppermute | solution.py:68
  3.6 88.4 %collective-permute-start.17 = (bf16[256,2048]{1,0:T(8,128)(2,1)}, bf16[256,2048]{1,0:T(8,128)(2,1)}, u32[]{:S(2)}, u32[]{:S(2)}) collective-permute-start(bf16[256,2048]{1,0:T(8,128)(2,1)} %bitcast.138), channel_id=1, source_target_pairs={{0,2},{2,6},{6,4},{4,0},{1,3},{3,7},{7,5},{5,1},{8,10},{10,14},{14... | collective-permute-start | bytes 3145736 | tf_op jit(solution)/shard_map/ppermute | solution.py:70
  10.8 27.1 %collective-permute-start = (bf16[512,768]{1,0:T(8,128)(2,1)}, bf16[512,768]{1,0:T(8,128)(2,1)}, u32[]{:S(2)}, u32[]{:S(2)}) collective-permute-start(bf16[512,768]{1,0:T(8,128)(2,1)} %maximum_maximum_fusion), channel_id=1, source_target_pairs={{0,0},{1,4},{2,2},{3,6},{4,1},{5,5},{6,3},{7,7},{8,8},{9,12},{10,1... | collective-permute-start | bytes 2359304 | tf_op jit(solution)/shard_map/ppermute | solution.py:107
  19.2 27.1 %collective-permute-start.2 = (bf16[512,768]{1,0:T(8,128)(2,1)}, bf16[512,768]{1,0:T(8,128)(2,1)}, u32[]{:S(2)}, u32[]{:S(2)}) collective-permute-start(bf16[512,768]{1,0:T(8,128)(2,1)} %maximum_maximum_fusion.1), channel_id=1, source_target_pairs={{0,2},{1,6},{2,0},{3,4},{4,3},{5,7},{6,1},{7,5},{8,10},{9,14},{10,... | collective-permute-start | bytes 2359304 | tf_op jit(solution)/shard_map/ppermute | solution.py:107
  21.8 27.8 %collective-permute-start.27 = (bf16[256,2048]{1,0:T(8,128)(2,1)}, bf16[256,2048]{1,0:T(8,128)(2,1)}, u32[]{:S(2)}, u32[]{:S(2)}) collective-permute-start(bf16[256,2048]{1,0:T(8,128)(2,1)} %bitcast.50), channel_id=1, source_target_pairs={{0,8},{8,0},{16,24},{24,16},{1,9},{9,1},{17,25},{25,17},{2,10},{10... | collective-permute-start | bytes 3145736 | tf_op jit(solution)/shard_map/ppermute | solution.py:77
  37.9 29.0 %collective-permute-start.4 = (bf16[512,768]{1,0:T(8,128)(2,1)}, bf16[512,768]{1,0:T(8,128)(2,1)S(1)}, u32[]{:S(2)}, u32[]{:S(2)}) collective-permute-start(bf16[512,768]{1,0:T(8,128)(2,1)} %maximum_maximum_fusion.2), channel_id=1, source_target_pairs={{0,16},{1,20},{2,18},{3,22},{4,17},{5,21},{6,19},{7,23},{8,24},{9,... | collective-permute-start | bytes 2359304 | tf_op jit(solution)/shard_map/ppermute | solution.py:107
  46.3 45.2 %collective-permute-start.6 = (bf16[512,768]{1,0:T(8,128)(2,1)}, bf16[512,768]{1,0:T(8,128)(2,1)S(1)}, u32[]{:S(2)}, u32[]{:S(2)}) collective-permute-start(bf16[512,768]{1,0:T(8,128)(2,1)} %maximum_maximum_fusion.3), channel_id=1, source_target_pairs={{0,18},{1,22},{2,16},{3,20},{4,19},{5,23},{6,17},{7,21},{8,26},{9,... | collective-permute-start | bytes 2359304 | tf_op jit(solution)/shard_map/ppermute | solution.py:107
  49.6 45.0 %collective-permute-start.1 = (bf16[512,768]{1,0:T(8,128)(2,1)}, bf16[512,768]{1,0:T(8,128)(2,1)S(1)}, u32[]{:S(2)}, u32[]{:S(2)}) collective-permute-start(bf16[512,768]{1,0:T(8,128)(2,1)} %collective-permute-done), channel_id=1, source_target_pairs={{0,1},{1,0},{2,3},{3,2},{4,5},{5,4},{6,7},{7,6},{8,9},{9,8},{10,11... | collective-permute-start | bytes 2359304 | tf_op jit(solution)/shard_map/ppermute | solution.py:115
  66.9 31.1 %collective-permute-start.3 = (bf16[512,768]{1,0:T(8,128)(2,1)}, bf16[512,768]{1,0:T(8,128)(2,1)S(1)}, u32[]{:S(2)}, u32[]{:S(2)}) collective-permute-start(bf16[512,768]{1,0:T(8,128)(2,1)} %collective-permute-done.2), channel_id=1, source_target_pairs={{0,1},{1,0},{2,3},{3,2},{4,5},{5,4},{6,7},{7,6},{8,9},{9,8},{10,11... | collective-permute-start | bytes 2359304 | tf_op jit(solution)/shard_map/ppermute | solution.py:115
  89.2 9.5 %collective-permute-start.5 = (bf16[512,768]{1,0:T(8,128)(2,1)S(1)}, bf16[512,768]{1,0:T(8,128)(2,1)S(1)}, u32[]{:S(2)}, u32[]{:S(2)}) collective-permute-start(bf16[512,768]{1,0:T(8,128)(2,1)S(1)} %collective-permute-done.4), channel_id=1, source_target_pairs={{0,1},{1,0},{2,3},{3,2},{4,5},{5,4},{6,7},{7,6},{8,9},{9,8},{10,11... | collective-permute-start | bytes 2359304 | tf_op jit(solution)/shard_map/ppermute | solution.py:115
  91.5 121.5 %collective-permute-start.8 = (bf16[2048,768]{1,0:T(8,128)(2,1)S(1)}, bf16[2048,768]{1,0:T(8,128)(2,1)S(1)}, u32[]{:S(2)}, u32[]{:S(2)}) collective-permute-start(bf16[2048,768]{1,0:T(8,128)(2,1)S(1)} %copy-done.3), channel_id=1, source_target_pairs={{0,16},{8,24},{16,0},{24,8},{1,17},{9,25},{17,1},{25,9},{2,18},{10... | collective-permute-start | bytes 9437192 | tf_op jit(solution)/shard_map/ppermute | solution.py:74
  92.0 12.7 %collective-permute-start.7 = (bf16[512,768]{1,0:T(8,128)(2,1)S(1)}, bf16[512,768]{1,0:T(8,128)(2,1)S(1)}, u32[]{:S(2)}, u32[]{:S(2)}) collective-permute-start(bf16[512,768]{1,0:T(8,128)(2,1)S(1)} %collective-permute-done.6), channel_id=1, source_target_pairs={{0,1},{1,0},{2,3},{3,2},{4,5},{5,4},{6,7},{7,6},{8,9},{9,8},{10,11... | collective-permute-start | bytes 2359304 | tf_op jit(solution)/shard_map/ppermute | solution.py:115
  94.6 112.4 %collective-permute-start.28 = (bf16[512,2048]{1,0:T(8,128)(2,1)S(1)}, bf16[512,2048]{1,0:T(8,128)(2,1)S(1)}, u32[]{:S(2)}, u32[]{:S(2)}) collective-permute-start(bf16[512,2048]{1,0:T(8,128)(2,1)S(1)} %pad_maximum_fusion.2), channel_id=1, source_target_pairs={{0,16},{8,24},{16,0},{24,8},{1,17},{9,25},{17,1},{25,9},{2,18},{10... | collective-permute-start | bytes 6291464 | tf_op jit(solution)/shard_map/ppermute | solution.py:78
  98.1 34.3 %collective-permute-start.18 = (bf16[256,2048]{1,0:T(8,128)(2,1)}, bf16[256,2048]{1,0:T(8,128)(2,1)S(1)}, u32[]{:S(2)}, u32[]{:S(2)}) collective-permute-start(bf16[256,2048]{1,0:T(8,128)(2,1)} %collective-permute-done.17), channel_id=1, source_target_pairs={{0,8},{8,0},{16,24},{24,16},{1,9},{9,1},{17,25},{25,17},{2,10},{10... | collective-permute-start | bytes 3145736 | tf_op jit(solution)/shard_map/ppermute | solution.py:68
  98.7 32.2 %collective-permute-start.19 = (bf16[256,2048]{1,0:T(8,128)(2,1)}, bf16[256,2048]{1,0:T(8,128)(2,1)S(1)}, u32[]{:S(2)}, u32[]{:S(2)}) collective-permute-start(bf16[256,2048]{1,0:T(8,128)(2,1)} %collective-permute-done.17), channel_id=1, source_target_pairs={{0,2},{2,6},{6,4},{4,0},{1,3},{3,7},{7,5},{5,1},{8,10},{10,14},{14... | collective-permute-start | bytes 3145736 | tf_op jit(solution)/shard_map/ppermute | solution.py:70
  104.8 27.9 %collective-permute-start.26 = (bf16[1024,512]{1,0:T(8,128)(2,1)S(1)}, bf16[1024,512]{1,0:T(8,128)(2,1)S(1)}, u32[]{:S(2)}, u32[]{:S(2)}) collective-permute-start(bf16[1024,512]{1,0:T(8,128)(2,1)S(1)} %copy-done.5), channel_id=1, source_target_pairs={{0,1},{1,0},{2,3},{3,2},{4,5},{5,4},{6,7},{7,6},{8,9},{9,8},{10,11... | collective-permute-start | bytes 3145736 | tf_op jit(solution)/shard_map/ppermute | solution.py:85
  130.9 81.9 %collective-permute-start.20 = (bf16[256,2048]{1,0:T(8,128)(2,1)S(1)}, bf16[256,2048]{1,0:T(8,128)(2,1)S(1)}, u32[]{:S(2)}, u32[]{:S(2)}) collective-permute-start(bf16[256,2048]{1,0:T(8,128)(2,1)S(1)} %collective-permute-done.19), channel_id=1, source_target_pairs={{0,8},{8,0},{16,24},{24,16},{1,9},{9,1},{17,25},{25,17},{2,10},{10... | collective-permute-start | bytes 3145736 | tf_op jit(solution)/shard_map/ppermute | solution.py:68
  132.4 79.9 %collective-permute-start.21 = (bf16[256,2048]{1,0:T(8,128)(2,1)S(1)}, bf16[256,2048]{1,0:T(8,128)(2,1)S(1)}, u32[]{:S(2)}, u32[]{:S(2)}) collective-permute-start(bf16[256,2048]{1,0:T(8,128)(2,1)S(1)} %collective-permute-done.19), channel_id=1, source_target_pairs={{0,2},{2,6},{6,4},{4,0},{1,3},{3,7},{7,5},{5,1},{8,10},{10,14},{14... | collective-permute-start | bytes 3145736 | tf_op jit(solution)/shard_map/ppermute | solution.py:70
  211.0 52.7 %collective-permute-start.29 = (bf16[256,2048]{1,0:T(8,128)(2,1)}, bf16[256,2048]{1,0:T(8,128)(2,1)}, u32[]{:S(2)}, u32[]{:S(2)}) collective-permute-start(bf16[256,2048]{1,0:T(8,128)(2,1)} %convolution_convert_fusion), channel_id=1, source_target_pairs={{0,2},{2,6},{6,4},{4,0},{1,3},{3,7},{7,5},{5,1},{8,10},{10,14},{14... | collective-permute-start | bytes 3145736 | tf_op jit(solution)/shard_map/ppermute | solution.py:129
  212.2 24.8 %collective-permute-start.22 = (bf16[256,2048]{1,0:T(8,128)(2,1)S(1)}, bf16[256,2048]{1,0:T(8,128)(2,1)S(1)}, u32[]{:S(2)}, u32[]{:S(2)}) collective-permute-start(bf16[256,2048]{1,0:T(8,128)(2,1)S(1)} %collective-permute-done.21), channel_id=1, source_target_pairs={{0,8},{8,0},{16,24},{24,16},{1,9},{9,1},{17,25},{25,17},{2,10},{10... | collective-permute-start | bytes 3145736 | tf_op jit(solution)/shard_map/ppermute | solution.py:68
  218.9 40.8 %collective-permute-start.12 = (bf16[256,2048]{1,0:T(8,128)(2,1)}, bf16[256,2048]{1,0:T(8,128)(2,1)}, u32[]{:S(2)}, u32[]{:S(2)}) collective-permute-start(bf16[256,2048]{1,0:T(8,128)(2,1)} %convolution_convert_fusion.1), channel_id=1, source_target_pairs={{0,8},{8,0},{16,24},{24,16},{1,9},{9,1},{17,25},{25,17},{2,10},{10... | collective-permute-start | bytes 3145736 | tf_op jit(solution)/shard_map/ppermute | solution.py:136
  220.4 71.0 %collective-permute-start.11 = (bf16[256,2048]{1,0:T(8,128)(2,1)}, bf16[256,2048]{1,0:T(8,128)(2,1)S(1)}, u32[]{:S(2)}, u32[]{:S(2)}) collective-permute-start(bf16[256,2048]{1,0:T(8,128)(2,1)} %convolution_convert_fusion.2), channel_id=1, source_target_pairs={{0,8},{8,0},{16,24},{24,16},{1,9},{9,1},{17,25},{25,17},{2,10},{10... | collective-permute-start | bytes 3145736 | tf_op jit(solution)/shard_map/ppermute | solution.py:136
  222.7 102.0 %collective-permute-start.10 = (bf16[256,2048]{1,0:T(8,128)(2,1)S(1)}, bf16[256,2048]{1,0:T(8,128)(2,1)S(1)}, u32[]{:S(2)}, u32[]{:S(2)}) collective-permute-start(bf16[256,2048]{1,0:T(8,128)(2,1)S(1)} %convolution_convert_fusion.3), channel_id=1, source_target_pairs={{0,8},{8,0},{16,24},{24,16},{1,9},{9,1},{17,25},{25,17},{2,10},{10... | collective-permute-start | bytes 3145736 | tf_op jit(solution)/shard_map/ppermute | solution.py:136
  237.1 132.3 %collective-permute-start.9 = (bf16[256,2048]{1,0:T(8,128)(2,1)S(1)}, bf16[256,2048]{1,0:T(8,128)(2,1)S(1)}, u32[]{:S(2)}, u32[]{:S(2)}) collective-permute-start(bf16[256,2048]{1,0:T(8,128)(2,1)S(1)} %convolution_convert_fusion.4), channel_id=1, source_target_pairs={{0,8},{8,0},{16,24},{24,16},{1,9},{9,1},{17,25},{25,17},{2,10},{10... | collective-permute-start | bytes 3145736 | tf_op jit(solution)/shard_map/ppermute | solution.py:136
  259.7 24.9 %collective-permute-start.23 = (bf16[2048,256]{1,0:T(8,128)(2,1)}, bf16[2048,256]{1,0:T(8,128)(2,1)}, u32[]{:S(2)}, u32[]{:S(2)}) collective-permute-start(bf16[2048,256]{1,0:T(8,128)(2,1)} %convolution_convert_fusion.7), channel_id=1, source_target_pairs={{0,16},{8,24},{16,0},{24,8},{1,17},{9,25},{17,1},{25,9},{2,18},{10... | collective-permute-start | bytes 3145736 | tf_op jit(solution)/shard_map/ppermute | solution.py:149
  263.7 30.9 %collective-permute-start.13 = (bf16[256,2048]{1,0:T(8,128)(2,1)}, bf16[256,2048]{1,0:T(8,128)(2,1)S(1)}, u32[]{:S(2)}, u32[]{:S(2)}) collective-permute-start(bf16[256,2048]{1,0:T(8,128)(2,1)} %fusion.6), channel_id=1, source_target_pairs={{0,2},{2,6},{6,4},{4,0},{1,3},{3,7},{7,5},{5,1},{8,10},{10,14},{14... | collective-permute-start | bytes 3145736 | tf_op jit(solution)/shard_map/ppermute | solution.py:141
  284.5 30.6 %collective-permute-start.30 = (bf16[256,2048]{1,0:T(8,128)(2,1)}, bf16[256,2048]{1,0:T(8,128)(2,1)}, u32[]{:S(2)}, u32[]{:S(2)}) collective-permute-start(bf16[256,2048]{1,0:T(8,128)(2,1)} %fusion.8), channel_id=1, source_target_pairs={{0,2},{2,6},{6,4},{4,0},{1,3},{3,7},{7,5},{5,1},{8,10},{10,14},{14... | collective-permute-start | bytes 3145736 | tf_op jit(solution)/shard_map/ppermute | solution.py:129
  291.4 27.9 %collective-permute-start.24 = (bf16[2048,256]{1,0:T(8,128)(2,1)}, bf16[2048,256]{1,0:T(8,128)(2,1)}, u32[]{:S(2)}, u32[]{:S(2)}) collective-permute-start(bf16[2048,256]{1,0:T(8,128)(2,1)} %convolution_convert_fusion.6), channel_id=1, source_target_pairs={{0,16},{8,24},{16,0},{24,8},{1,17},{9,25},{17,1},{25,9},{2,18},{10... | collective-permute-start | bytes 3145736 | tf_op jit(solution)/shard_map/ppermute | solution.py:149
  295.5 50.1 %collective-permute-start.25 = (bf16[2048,256]{1,0:T(8,128)(2,1)S(1)}, bf16[2048,256]{1,0:T(8,128)(2,1)}, u32[]{:S(2)}, u32[]{:S(2)}) collective-permute-start(bf16[2048,256]{1,0:T(8,128)(2,1)S(1)} %convolution_convert_fusion.5), channel_id=1, source_target_pairs={{0,16},{8,24},{16,0},{24,8},{1,17},{9,25},{17,1},{25,9},{2,18},{10... | collective-permute-start | bytes 3145736 | tf_op jit(solution)/shard_map/ppermute | solution.py:149
  315.1 27.3 %collective-permute-start.14 = (bf16[256,2048]{1,0:T(8,128)(2,1)}, bf16[256,2048]{1,0:T(8,128)(2,1)}, u32[]{:S(2)}, u32[]{:S(2)}) collective-permute-start(bf16[256,2048]{1,0:T(8,128)(2,1)} %fusion.5), channel_id=1, source_target_pairs={{0,2},{2,6},{6,4},{4,0},{1,3},{3,7},{7,5},{5,1},{8,10},{10,14},{14... | collective-permute-start | bytes 3145736 | tf_op jit(solution)/shard_map/ppermute | solution.py:141
  319.3 45.6 %collective-permute-start.31 = (bf16[256,2048]{1,0:T(8,128)(2,1)}, bf16[256,2048]{1,0:T(8,128)(2,1)}, u32[]{:S(2)}, u32[]{:S(2)}) collective-permute-start(bf16[256,2048]{1,0:T(8,128)(2,1)} %fusion.7), channel_id=1, source_target_pairs={{0,2},{2,6},{6,4},{4,0},{1,3},{3,7},{7,5},{5,1},{8,10},{10,14},{14... | collective-permute-start | bytes 3145736 | tf_op jit(solution)/shard_map/ppermute | solution.py:129
  345.6 38.8 %collective-permute-start.15 = (bf16[256,2048]{1,0:T(8,128)(2,1)S(1)}, bf16[256,2048]{1,0:T(8,128)(2,1)S(1)}, u32[]{:S(2)}, u32[]{:S(2)}) collective-permute-start(bf16[256,2048]{1,0:T(8,128)(2,1)S(1)} %fusion.4), channel_id=1, source_target_pairs={{0,2},{2,6},{6,4},{4,0},{1,3},{3,7},{7,5},{5,1},{8,10},{10,14},{14... | collective-permute-start | bytes 3145736 | tf_op jit(solution)/shard_map/ppermute | solution.py:141
  (11 other events, 364.8 us)

commit v2 on v1

--- a/solution.py
+++ b/solution.py
@@ -61,21 +61,18 @@
         place = ring_place(j, nj)
         grads = (grad_query, grad_key, grad_value)
 
-        rows = inputs.reshape(tok, width)
-        blocks = []
-        for step in range(nj):
-            blocks.append(rows)
-            blocks.append(lax.ppermute(rows, "ia", swap_x))
-            if step < nj - 1:
-                rows = lax.ppermute(rows, "ja", ring)
-        x_all = jnp.concatenate(blocks, axis=0)
-
-        w_own = jnp.concatenate((query_weight, key_weight, value_weight), axis=1)
-        w_both = jnp.concatenate((w_own, lax.ppermute(w_own, "ia", swap_y)), axis=1)
+        def after(value, *earlier):
+            return lax.optimization_barrier((value, *earlier))[0]
 
         go_own = grad_out.reshape(tok, width)
         go_pair = jnp.concatenate((go_own, lax.ppermute(go_own, "ia", swap_x)), axis=0)
+
+        weights = (query_weight, key_weight, value_weight)
+        others = [lax.ppermute(query_weight, "ia", swap_y)]
         go_all = jnp.concatenate((go_pair, lax.ppermute(go_pair, "ia", swap_y)), axis=0)
+        others.append(lax.ppermute(after(key_weight, others[0]), "ia", swap_y))
+        others.append(lax.ppermute(after(value_weight, go_all), "ia", swap_y))
+        w_both = jnp.concatenate((*weights, *others), axis=1)
 
         attn = jnp.concatenate(
             [lax.dynamic_index_in_dim(attn_out, i ^ r, 0, keepdims=False) for r in range(ni)], axis=0
@@ -85,34 +82,44 @@
             attn_list.append(lax.ppermute(attn_list[-1], "ka", core_ring))
         attn_all = jnp.stack(attn_list)
 
-        g_all = jnp.zeros((nj, 2 * tok, 6 * feat), BF16)
-        for dy in range(2):
-            for step in range(per):
-                chunk = (j + step) % per
-                piece = jnp.concatenate(
-                    [
-                        jnp.concatenate(
-                            [
-                                lax.dynamic_slice(
-                                    grad, (i ^ (2 * dy) ^ dx, 0, chunk * feat), (1, tok, feat)
-                                ).reshape(tok, feat)
-                                for grad in grads
-                            ],
-                            axis=1,
-                        )
-                        for dx in range(2)
-                    ],
-                    axis=0,
-                )
-                piece = lax.ppermute(piece, ("ia", "ja", "ka"), deal_pairs(step, dy))
-                for hop in range(nk):
-                    source = per * ((k - hop) % nk) + (j % per - step) % per
-                    slot = (place - ring_place(source, nj)) % nj
-                    g_all = lax.dynamic_update_slice(
-                        g_all, piece[None], (slot, 0, dy * 3 * feat)
+        def deal_piece(step, dy):
+            chunk = (j + step) % per
+            return jnp.concatenate(
+                [
+                    jnp.concatenate(
+                        [
+                            lax.dynamic_slice(
+                                grad, (i ^ (2 * dy) ^ dx, 0, chunk * feat), (1, tok, feat)
+                            ).reshape(tok, feat)
+                            for grad in grads
+                        ],
+                        axis=1,
                     )
-                    if hop < nk - 1:
-                        piece = lax.ppermute(piece, "ka", core_ring)
+                    for dx in range(2)
+                ],
+                axis=0,
+            )
+
+        deals = [(step, dy) for step in range(per) for dy in range(2)]
+        rows = inputs.reshape(tok, width)
+        blocks = [rows, lax.ppermute(after(rows, go_pair), "ia", swap_x)]
+        dealt = []
+        queue = [rows, rows]
+
+        def send_deal():
+            step, dy = deals[len(dealt)]
+            piece = after(deal_piece(step, dy), queue[-2])
+            dealt.append(lax.ppermute(piece, ("ia", "ja", "ka"), deal_pairs(step, dy)))
+            queue.append(dealt[-1])
+
+        for step in range(1, nj):
+            rows = lax.ppermute(after(rows, queue[-2]), "ja", ring)
+            queue.append(rows)
+            blocks.append(rows)
+            blocks.append(lax.ppermute(rows, "ia", swap_x))
+            if len(dealt) < len(deals) and step < nj:
+                send_deal()
+        x_all = jnp.concatenate(blocks, axis=0)
 
         def output_chunk(step):
             back = (place - step) % nj
@@ -124,23 +131,48 @@
             )
             return dot_rows(part.reshape(ni * tok, feat), go_all)
 
-        moving = output_chunk(1).astype(BF16)
+        state = {"step": 1, "moving": output_chunk(1).astype(BF16)}
+
+        def send_output():
+            moving = lax.ppermute(after(state["moving"], queue[-2]), "ja", ring)
+            queue.append(moving)
+            state["step"] += 1
+            state["total"] = output_chunk(state["step"] % nj) + moving.astype(F32)
+            state["moving"] = state["total"].astype(BF16)
+
+        send_output()
+        while len(dealt) < len(deals):
+            send_deal()
+
+        g_all = jnp.zeros((nj, 2 * tok, 6 * feat), BF16)
+        for (step, dy), piece in zip(deals, dealt):
+            for hop in range(nk):
+                source = per * ((k - hop) % nk) + (j % per - step) % per
+                slot = (place - ring_place(source, nj)) % nj
+                g_all = lax.dynamic_update_slice(g_all, piece[None], (slot, 0, dy * 3 * feat))
+                if hop < nk - 1:
+                    piece = lax.ppermute(piece, "ka", core_ring)
+
+        others = []
+        for step in range(1, nj + 1):
+            other = dot_cols(g_all[step % nj, tok:], w_both).astype(BF16)
+            if step > 2:
+                other = after(other, others[step - 3])
+            others.append(lax.ppermute(other, "ia", swap_x))
+
+        def input_chunk(step):
+            return dot_cols(g_all[step % nj, :tok], w_both) + others[step - 1].astype(F32)
+
+        send_output()
+        summed = input_chunk(1).astype(BF16)
         for step in range(1, nj):
-            moving = lax.ppermute(moving, "ja", ring)
-            total = output_chunk((step + 1) % nj) + moving.astype(F32)
-            moving = total.astype(BF16)
-        output_weight_grad = total
-
-        def input_chunk(step):
-            other = dot_cols(g_all[step % nj, tok:], w_both).astype(BF16)
-            other = lax.ppermute(other, "ia", swap_x)
-            return dot_cols(g_all[step % nj, :tok], w_both) + other.astype(F32)
-
-        moving = input_chunk(1).astype(BF16)
-        for step in range(1, nj):
-            moving = lax.ppermute(moving, "ja", ring)
-            moving = (input_chunk(step + 1) + moving.astype(F32)).astype(BF16)
-        grad_inputs = moving.reshape(inputs.shape)
+            summed = lax.ppermute(after(summed, queue[-2]), "ja", ring)
+            queue.append(summed)
+            summed = (input_chunk(step + 1) + summed.astype(F32)).astype(BF16)
+            if state["step"] < nj:
+                send_output()
+        grad_inputs = summed.reshape(inputs.shape)
+        output_weight_grad = state["total"]
 
         g_flat = g_all.reshape(nj * 2 * tok, 6 * feat)
         weight_grads = []

time: 394 us -> 395 us (level)
  waiting for transfers between devices: 203 us -> 229 us
  starting transfers between devices: 81.1 us -> 60.1 us
    ppermute x18 -> x21, waiting for transfers between devices: 106 us -> 227 us  [the longest x1 55.2 us: local(): others.append(lax.ppermute(after(value_weight, go_all), 'ia', swap_y))]
    ppermute x1, waiting for transfers between devices: 74.3 us -> 0.01 us  [local(): lax.ppermute(go_pair, 'ia', swap_y)]
    ppermute x4, starting transfers between devices: 36.3 us -> 12.3 us  [local(): piece = lax.ppermute(piece, 'ka', core_ring)]
    ppermute x3, waiting for transfers between devices: 11.7 us -> 0.01 us  [local(): other = lax.ppermute(other, 'ia', swap_y)]
    ppermute x4 -> x3, waiting for transfers between devices: 11 us -> 0.01 us  [local(): blocks.append(lax.ppermute(rows, 'ia', swap_x))]
    ppermute x18 -> x21, starting transfers between devices: 35 us -> 37 us  [the longest x3 12 us: send_output(): moving = lax.ppermute(after(state['moving'], queue[-2]), 'ja', ring)]
    unnamed x32 -> x38, local copies, waits for them, and re-layouts: 12.5 us -> 12.4 us
  transfers between devices with their start and end apart: 32 -> 34, of which waited for: 12 -> 12; matrix products, arithmetic and copies ran while one was open for 25% -> 24% of each run, Pallas kernels for 0% -> 0%
where the time goes in v2:
time: 395 us; the launch traced here: 390 us
  waiting for transfers between devices  229 us (58%)
  matrix products  66.5 us (17%)
  starting transfers between devices  60.1 us (15%)
  local copies, waits for them, and re-layouts  22.1 us (6%)
  other arithmetic  9.95 us (3%)
    ppermute x1, waiting for transfers between devices, local(): others.append(lax.ppermute(after(value_weight, go_all), 'ia', swap_y))  55.2 us
    ppermute x3, waiting for transfers between devices, local(): summed = lax.ppermute(after(summed, queue[-2]), 'ja', ring)  43.9 us
    dot_general x10, matrix products, dot_rows(): lax.dot_general(a, b, (((0,), (0,)), ((), ())), preferred_element_type=F32)  41 us
    ppermute x3, waiting for transfers between devices, local(): rows = lax.ppermute(after(rows, queue[-2]), 'ja', ring)  38.5 us
    ppermute x3, waiting for transfers between devices, send_output(): moving = lax.ppermute(after(state['moving'], queue[-2]), 'ja', ring)  31.9 us
    ppermute x4, waiting for transfers between devices, local(): others.append(lax.ppermute(other, 'ia', swap_x))  31.4 us
    dot_general x8, matrix products, dot_cols(): lax.dot_general(a, b, (((1,), (1,)), ((), ())), preferred_element_type=F32)  25.5 us
    ppermute x4, waiting for transfers between devices, send_deal(): dealt.append(lax.ppermute(piece, ('ia', 'ja', 'ka'), deal_pairs(step, dy)))  15.8 us
  transfers between devices with their start and end apart: 34, of which 12 were waited for; matrix products, arithmetic and copies ran while one was open for 24% of the time, Pallas kernels for 0%

profile of v2, /device:TPU:0, one launch (start us, length us, event | category | flops | bytes accessed | tf_op | source)
XLA Modules:
  0.0 389.5 jit_solution(4284100932641252636)
XLA Ops:
  0.7 3.0 collective-permute-start.10
  11.0 7.4 %collective-permute-start = (bf16[512,768]{1,0:T(8,128)(2,1)}, bf16[512,768]{1,0:T(8,128)(2,1)}, u32[]{:S(2)}, u32[]{:S(2)}) collective-permute-start(bf16[512,768]{1,0:T(8,128)(2,1)} %maximum_maximum_fusion), channel_id=1, source_target_pairs={{0,0},{1,4},{2,2},{3,6},{4,1},{5,5},{6,3},{7,7},{8,8},{9,12},{10,1... | collective-permute-start | bytes 2359304 | tf_op jit(solution)/shard_map/ppermute | solution.py:112
  34.8 12.2 %collective-permute-start.1 = (bf16[512,768]{1,0:T(8,128)(2,1)}, bf16[512,768]{1,0:T(8,128)(2,1)}, u32[]{:S(2)}, u32[]{:S(2)}) collective-permute-start(bf16[512,768]{1,0:T(8,128)(2,1)} %collective-permute-done), channel_id=1, source_target_pairs={{0,1},{1,0},{2,3},{3,2},{4,5},{5,4},{6,7},{7,6},{8,9},{9,8},{10,11... | collective-permute-start | bytes 2359304 | tf_op jit(solution)/shard_map/ppermute | solution.py:154
  49.3 4.7 %collective-permute-start.21 = (bf16[256,2048]{1,0:T(8,128)(2,1)}, bf16[256,2048]{1,0:T(8,128)(2,1)S(1)}, u32[]{:S(2)}, u32[]{:S(2)}) collective-permute-start(bf16[256,2048]{1,0:T(8,128)(2,1)} %collective-permute-done.20), channel_id=1, source_target_pairs={{0,2},{2,6},{6,4},{4,0},{1,3},{3,7},{7,5},{5,1},{8,10},{10,14},{14... | collective-permute-start | bytes 3145736 | tf_op jit(solution)/shard_map/ppermute | solution.py:116
  64.5 10.6 %collective-permute-done.27 = bf16[256,2048]{1,0:T(8,128)(2,1)} collective-permute-done((bf16[256,2048]{1,0:T(8,128)(2,1)}, bf16[256,2048]{1,0:T(8,128)(2,1)}, u32[]{:S(2)}, u32[]{:S(2)}) %collective-permute-start.27) | collective-permute-done | bytes 1048608 | tf_op jit(solution)/shard_map/ppermute | solution.py:105
  77.1 22.0 %collective-permute-done.21 = bf16[256,2048]{1,0:T(8,128)(2,1)S(1)} collective-permute-done((bf16[256,2048]{1,0:T(8,128)(2,1)}, bf16[256,2048]{1,0:T(8,128)(2,1)S(1)}, u32[]{:S(2)}, u32[]{:S(2)}) %collective-permute-start.21) | collective-permute-done | bytes 1048608 | tf_op jit(solution)/shard_map/ppermute | solution.py:116
  101.4 55.2 %collective-permute-done.12 = bf16[2048,256]{1,0:T(8,128)(2,1)S(1)} collective-permute-done((bf16[2048,256]{1,0:T(8,128)(2,1)S(1)}, bf16[2048,256]{1,0:T(8,128)(2,1)S(1)}, u32[]{:S(2)}, u32[]{:S(2)}) %collective-permute-start.12) | collective-permute-done | bytes 1048608 | tf_op jit(solution)/shard_map/ppermute | solution.py:74
  157.5 3.9 %collective-permute-start.6 = (bf16[512,768]{1,0:T(8,128)(2,1)S(1)}, bf16[512,768]{1,0:T(8,128)(2,1)S(1)}, u32[]{:S(2)}, u32[]{:S(2)}) collective-permute-start(bf16[512,768]{1,0:T(8,128)(2,1)S(1)} %copy-done.7), channel_id=1, source_target_pairs={{0,18},{1,22},{2,16},{3,20},{4,19},{5,23},{6,17},{7,21},{8,26},{9,... | collective-permute-start | bytes 2359304 | tf_op jit(solution)/shard_map/ppermute | solution.py:112
  161.7 3.3 convolution_convert_fusion
  165.0 16.4 %collective-permute-done.22 = bf16[256,2048]{1,0:T(8,128)(2,1)S(1)} collective-permute-done((bf16[256,2048]{1,0:T(8,128)(2,1)S(1)}, bf16[256,2048]{1,0:T(8,128)(2,1)S(1)}, u32[]{:S(2)}, u32[]{:S(2)}) %collective-permute-start.22) | collective-permute-done | bytes 1048608 | tf_op jit(solution)/shard_map/ppermute | solution.py:116
  181.4 8.0 %collective-permute-start.23 = (bf16[256,2048]{1,0:T(8,128)(2,1)S(1)}, bf16[256,2048]{1,0:T(8,128)(2,1)}, u32[]{:S(2)}, u32[]{:S(2)}) collective-permute-start(bf16[256,2048]{1,0:T(8,128)(2,1)S(1)} %convolution_convert_fusion), channel_id=1, source_target_pairs={{0,2},{2,6},{6,4},{4,0},{1,3},{3,7},{7,5},{5,1},{8,10},{10,14},{14... | collective-permute-start | bytes 3145736 | tf_op jit(solution)/shard_map/ppermute | solution.py:137
  190.1 15.8 %collective-permute-done.6 = bf16[512,768]{1,0:T(8,128)(2,1)S(1)} collective-permute-done((bf16[512,768]{1,0:T(8,128)(2,1)S(1)}, bf16[512,768]{1,0:T(8,128)(2,1)S(1)}, u32[]{:S(2)}, u32[]{:S(2)}) %collective-permute-start.6) | collective-permute-done | bytes 786464 | tf_op jit(solution)/shard_map/ppermute | solution.py:112
  208.3 2.8 convolution_convert_fusion.3
  219.7 3.6 convolution_convert_fusion.5
  223.4 3.6 convolution_convert_fusion.6
  227.5 2.9 convolution_convert_fusion.7
  230.5 31.4 %collective-permute-done.15 = bf16[256,2048]{1,0:T(8,128)(2,1)} collective-permute-done((bf16[256,2048]{1,0:T(8,128)(2,1)}, bf16[256,2048]{1,0:T(8,128)(2,1)}, u32[]{:S(2)}, u32[]{:S(2)}) %collective-permute-start.15) | collective-permute-done | bytes 1048608 | tf_op jit(solution)/shard_map/ppermute | solution.py:161
  261.9 4.0 %fusion.6 = bf16[256,2048]{1,0:T(8,128)(2,1)} fusion(bf16[2048,1536]{1,0:T(8,128)(2,1)S(1)} %constant_dynamic-update-slice_fusion, bf16[256,2048]{1,0:T(8,128)(2,1)} %collective-permute-done.15, bf16[4,512,1536]{2,1,0:T(8,128)(2,1)S(1)} %bitcast_dynamic-update-slice_fusion), kind=kOutput, calls=%fused_computation.25 | convolution fusion | flops 1612185600 | bytes 9175040 | tf_op jit(solution)/shard_map/dot_general | solution.py:24
  266.3 3.8 fusion.8
  274.1 5.2 %convolution_add_fusion.3 = f32[2048,256]{1,0:T(8,128)} fusion(bf16[2048,2048]{1,0:T(8,128)(2,1)S(1)} %constant_dynamic-update-slice_fusion.6, bf16[2048,256]{1,0:T(8,128)(2,1)} %collective-permute-done.33, bf16[2048,1536]{1,0:T(8,128)(2,1)S(1)} %bitcast.134), kind=kOutput, calls=%fused_computation.12 | convolution fusion | flops 2148532224 | bytes 12582912 | tf_op jit(solution)/shard_map/dot_general | solution.py:20
  279.3 14.0 %collective-permute-done.17 = bf16[256,2048]{1,0:T(8,128)(2,1)} collective-permute-done((bf16[256,2048]{1,0:T(8,128)(2,1)}, bf16[256,2048]{1,0:T(8,128)(2,1)}, u32[]{:S(2)}, u32[]{:S(2)}) %collective-permute-start.17) | collective-permute-done | bytes 1048608 | tf_op jit(solution)/shard_map/ppermute | solution.py:169
  294.1 4.4 %fusion.5 = bf16[256,2048]{1,0:T(8,128)(2,1)} fusion(bf16[2048,1536]{1,0:T(8,128)(2,1)S(1)} %constant_dynamic-update-slice_fusion, bf16[256,2048]{1,0:T(8,128)(2,1)} %collective-permute-done.17, bf16[256,2048]{1,0:T(8,128)(2,1)} %collective-permute-done.13, bf16[4,512,1536]{2,1,0:T(8,128)(2,1)S(1)} %bitcast_dynamic-update-slice_fusion), kind=kOutput, calls=%fused_computation.24 | convolution fusion | flops 1613234176 | bytes 10223616 | tf_op jit(solution)/shard_map/dot_general | solution.py:24
  298.5 15.5 %collective-permute-done.24 = bf16[256,2048]{1,0:T(8,128)(2,1)} collective-permute-done((bf16[256,2048]{1,0:T(8,128)(2,1)}, bf16[256,2048]{1,0:T(8,128)(2,1)}, u32[]{:S(2)}, u32[]{:S(2)}) %collective-permute-start.24) | collective-permute-done | bytes 1048608 | tf_op jit(solution)/shard_map/ppermute | solution.py:137
  314.0 3.8 fusion.7
  320.3 5.2 %convolution_add_fusion.4 = f32[2048,256]{1,0:T(8,128)} fusion(bf16[2048,2048]{1,0:T(8,128)(2,1)S(1)} %constant_dynamic-update-slice_fusion.6, bf16[2048,256]{1,0:T(8,128)(2,1)} %collective-permute-done.32, bf16[2048,1536]{1,0:T(8,128)(2,1)S(1)} %bitcast.135), kind=kOutput, calls=%fused_computation.13 | convolution fusion | flops 2148532224 | bytes 12582912 | tf_op jit(solution)/shard_map/dot_general | solution.py:20
  325.5 15.8 %collective-permute-done.18 = bf16[256,2048]{1,0:T(8,128)(2,1)} collective-permute-done((bf16[256,2048]{1,0:T(8,128)(2,1)}, bf16[256,2048]{1,0:T(8,128)(2,1)}, u32[]{:S(2)}, u32[]{:S(2)}) %collective-permute-start.18) | collective-permute-done | bytes 1048608 | tf_op jit(solution)/shard_map/ppermute | solution.py:169
  341.3 3.4 fusion.4
  344.8 16.4 %collective-permute-done.25 = bf16[256,2048]{1,0:T(8,128)(2,1)} collective-permute-done((bf16[256,2048]{1,0:T(8,128)(2,1)}, bf16[256,2048]{1,0:T(8,128)(2,1)}, u32[]{:S(2)}, u32[]{:S(2)}) %collective-permute-start.25) | collective-permute-done | bytes 1048608 | tf_op jit(solution)/shard_map/ppermute | solution.py:137
  361.1 5.2 %convolution_add_fusion.5 = f32[2048,256]{1,0:T(8,128)} fusion(bf16[2048,2048]{1,0:T(8,128)(2,1)S(1)} %constant_dynamic-update-slice_fusion.6, bf16[2048,256]{1,0:T(8,128)(2,1)} %collective-permute-done.31, bf16[2048,1536]{1,0:T(8,128)(2,1)S(1)} %bitcast.136), kind=kOutput, calls=%fused_computation.14 | convolution fusion | flops 2148532224 | bytes 12582912 | tf_op jit(solution)/shard_map/dot_general | solution.py:20
  366.4 4.2 %convolution_add_fusion = f32[256,2048]{1,0:T(8,128)} fusion(bf16[256,2048]{1,0:T(8,128)(2,1)} %collective-permute-done.25, s32[]{:T(128)S(6)} %select_n.473, s32[]{:T(128)S(6)} %select_n.475, bf16[1,1024,512]{2,1,0:T(8,128)(2,1)S(1)} %get-tuple-element.42, bf16[1,1024,512]{2,1,0:T(8,128)(2,1)S(1)} %bitcast.148, bf16[512,2048]{1,0:T(8,128)(2,1)S(1)} %copy-done.12, ...), kind=kOutput, calls=%fused_computation.9 | convolution fusion | flops 1088421888 | bytes 9437192 | tf_op jit(solution)/shard_map/dot_general | solution.py:20
  370.5 14.1 %collective-permute-done.26 = bf16[256,2048]{1,0:T(8,128)(2,1)} collective-permute-done((bf16[256,2048]{1,0:T(8,128)(2,1)S(1)}, bf16[256,2048]{1,0:T(8,128)(2,1)}, u32[]{:S(2)}, u32[]{:S(2)}) %collective-permute-start.26) | collective-permute-done | bytes 1048608 | tf_op jit(solution)/shard_map/ppermute | solution.py:169
  384.7 4.4 %fusion.9 = bf16[1,256,2048]{2,1,0:T(8,128)(2,1)} fusion(bf16[2048,1536]{1,0:T(8,128)(2,1)S(1)} %constant_dynamic-update-slice_fusion, bf16[256,2048]{1,0:T(8,128)(2,1)} %collective-permute-done.26, bf16[256,2048]{1,0:T(8,128)(2,1)} %collective-permute-done.14, bf16[4,512,1536]{2,1,0:T(8,128)(2,1)S(1)} %bitcast_dynamic-update-slice_fusion), kind=kOutput, calls=%fused_computation.36 | convolution fusion | flops 1613234176 | bytes 10223616 | tf_op jit(solution)/shard_map/dot_general | solution.py:24
  (112 shorter events, 61.4 us)
Async XLA Ops:
  0.7 46.3 %collective-permute-start.10 = (bf16[256,2048]{1,0:T(8,128)(2,1)}, bf16[256,2048]{1,0:T(8,128)(2,1)}, u32[]{:S(2)}, u32[]{:S(2)}) collective-permute-start(bf16[256,2048]{1,0:T(8,128)(2,1)} %bitcast.139), channel_id=1, source_target_pairs={{0,8},{8,0},{16,24},{24,16},{1,9},{9,1},{17,25},{25,17},{2,10},{10... | collective-permute-start | bytes 3145736 | tf_op jit(solution)/shard_map/ppermute | solution.py:68
  3.7 45.6 %collective-permute-start.20 = (bf16[256,2048]{1,0:T(8,128)(2,1)}, bf16[256,2048]{1,0:T(8,128)(2,1)}, u32[]{:S(2)}, u32[]{:S(2)}) collective-permute-start(bf16[256,2048]{1,0:T(8,128)(2,1)} %bitcast.137), channel_id=1, source_target_pairs={{0,2},{2,6},{6,4},{4,0},{1,3},{3,7},{7,5},{5,1},{8,10},{10,14},{14... | collective-permute-start | bytes 3145736 | tf_op jit(solution)/shard_map/ppermute | solution.py:116
  18.4 37.3 %collective-permute-start.8 = (bf16[2048,256]{1,0:T(8,128)(2,1)}, bf16[2048,256]{1,0:T(8,128)(2,1)}, u32[]{:S(2)}, u32[]{:S(2)}) collective-permute-start(bf16[2048,256]{1,0:T(8,128)(2,1)} %param.15), channel_id=1, source_target_pairs={{0,16},{8,24},{16,0},{24,8},{1,17},{9,25},{17,1},{25,9},{2,18},{10... | collective-permute-start | bytes 3145736 | tf_op jit(solution)/shard_map/ppermute | solution.py:71
  34.3 27.4 %collective-permute-start.2 = (bf16[512,768]{1,0:T(8,128)(2,1)}, bf16[512,768]{1,0:T(8,128)(2,1)}, u32[]{:S(2)}, u32[]{:S(2)}) collective-permute-start(bf16[512,768]{1,0:T(8,128)(2,1)} %maximum_maximum_fusion.1), channel_id=1, source_target_pairs={{0,16},{1,20},{2,18},{3,22},{4,17},{5,21},{6,19},{7,23},{8,24},{9,... | collective-permute-start | bytes 2359304 | tf_op jit(solution)/shard_map/ppermute | solution.py:112
  34.8 24.9 %collective-permute-start.1 = (bf16[512,768]{1,0:T(8,128)(2,1)}, bf16[512,768]{1,0:T(8,128)(2,1)}, u32[]{:S(2)}, u32[]{:S(2)}) collective-permute-start(bf16[512,768]{1,0:T(8,128)(2,1)} %collective-permute-done), channel_id=1, source_target_pairs={{0,1},{1,0},{2,3},{3,2},{4,5},{5,4},{6,7},{7,6},{8,9},{9,8},{10,11... | collective-permute-start | bytes 2359304 | tf_op jit(solution)/shard_map/ppermute | solution.py:154
  48.6 26.4 %collective-permute-start.27 = (bf16[256,2048]{1,0:T(8,128)(2,1)}, bf16[256,2048]{1,0:T(8,128)(2,1)}, u32[]{:S(2)}, u32[]{:S(2)}) collective-permute-start(bf16[256,2048]{1,0:T(8,128)(2,1)} %bitcast.138), channel_id=1, source_target_pairs={{0,8},{8,0},{16,24},{24,16},{1,9},{9,1},{17,25},{25,17},{2,10},{10... | collective-permute-start | bytes 3145736 | tf_op jit(solution)/shard_map/ppermute | solution.py:105
  49.3 49.9 %collective-permute-start.21 = (bf16[256,2048]{1,0:T(8,128)(2,1)}, bf16[256,2048]{1,0:T(8,128)(2,1)S(1)}, u32[]{:S(2)}, u32[]{:S(2)}) collective-permute-start(bf16[256,2048]{1,0:T(8,128)(2,1)} %collective-permute-done.20), channel_id=1, source_target_pairs={{0,2},{2,6},{6,4},{4,0},{1,3},{3,7},{7,5},{5,1},{8,10},{10,14},{14... | collective-permute-start | bytes 3145736 | tf_op jit(solution)/shard_map/ppermute | solution.py:116
  55.7 44.8 %collective-permute-start.28 = (bf16[256,2048]{1,0:T(8,128)(2,1)}, bf16[256,2048]{1,0:T(8,128)(2,1)S(1)}, u32[]{:S(2)}, u32[]{:S(2)}) collective-permute-start(bf16[256,2048]{1,0:T(8,128)(2,1)} %collective-permute-done.20), channel_id=1, source_target_pairs={{0,8},{8,0},{16,24},{24,16},{1,9},{9,1},{17,25},{25,17},{2,10},{10... | collective-permute-start | bytes 3145736 | tf_op jit(solution)/shard_map/ppermute | solution.py:119
  59.7 41.0 %collective-permute-start.9 = (bf16[2048,256]{1,0:T(8,128)(2,1)S(1)}, bf16[2048,256]{1,0:T(8,128)(2,1)S(1)}, u32[]{:S(2)}, u32[]{:S(2)}) collective-permute-start(bf16[2048,256]{1,0:T(8,128)(2,1)S(1)} %copy-done.4), channel_id=1, source_target_pairs={{0,16},{8,24},{16,0},{24,8},{1,17},{9,25},{17,1},{25,9},{2,18},{10... | collective-permute-start | bytes 3145736 | tf_op jit(solution)/shard_map/ppermute | solution.py:73
  61.7 99.9 %collective-permute-start.11 = (bf16[512,2048]{1,0:T(8,128)(2,1)S(1)}, bf16[512,2048]{1,0:T(8,128)(2,1)S(1)}, u32[]{:S(2)}, u32[]{:S(2)}) collective-permute-start(bf16[512,2048]{1,0:T(8,128)(2,1)S(1)} %pad_maximum_fusion.1), channel_id=1, source_target_pairs={{0,16},{8,24},{16,0},{24,8},{1,17},{9,25},{17,1},{25,9},{2,18},{10... | collective-permute-start | bytes 6291464 | tf_op jit(solution)/shard_map/ppermute | solution.py:72
  75.1 81.6 %collective-permute-start.12 = (bf16[2048,256]{1,0:T(8,128)(2,1)S(1)}, bf16[2048,256]{1,0:T(8,128)(2,1)S(1)}, u32[]{:S(2)}, u32[]{:S(2)}) collective-permute-start(bf16[2048,256]{1,0:T(8,128)(2,1)S(1)} %copy-done.5), channel_id=1, source_target_pairs={{0,16},{8,24},{16,0},{24,8},{1,17},{9,25},{17,1},{25,9},{2,18},{10... | collective-permute-start | bytes 3145736 | tf_op jit(solution)/shard_map/ppermute | solution.py:74
  99.2 57.5 %collective-permute-start.4 = (bf16[512,768]{1,0:T(8,128)(2,1)S(1)}, bf16[512,768]{1,0:T(8,128)(2,1)S(1)}, u32[]{:S(2)}, u32[]{:S(2)}) collective-permute-start(bf16[512,768]{1,0:T(8,128)(2,1)S(1)} %copy-done.8), channel_id=1, source_target_pairs={{0,2},{1,6},{2,0},{3,4},{4,3},{5,7},{6,1},{7,5},{8,10},{9,14},{10,... | collective-permute-start | bytes 2359304 | tf_op jit(solution)/shard_map/ppermute | solution.py:112
  100.5 57.0 %collective-permute-start.3 = (bf16[512,768]{1,0:T(8,128)(2,1)}, bf16[512,768]{1,0:T(8,128)(2,1)S(1)}, u32[]{:S(2)}, u32[]{:S(2)}) collective-permute-start(bf16[512,768]{1,0:T(8,128)(2,1)} %collective-permute-done.2), channel_id=1, source_target_pairs={{0,1},{1,0},{2,3},{3,2},{4,5},{5,4},{6,7},{7,6},{8,9},{9,8},{10,11... | collective-permute-start | bytes 2359304 | tf_op jit(solution)/shard_map/ppermute | solution.py:154
  100.7 60.9 %collective-permute-start.19 = (bf16[1024,512]{1,0:T(8,128)(2,1)S(1)}, bf16[1024,512]{1,0:T(8,128)(2,1)S(1)}, u32[]{:S(2)}, u32[]{:S(2)}) collective-permute-start(bf16[1024,512]{1,0:T(8,128)(2,1)S(1)} %copy-done), channel_id=1, source_target_pairs={{0,1},{1,0},{2,3},{3,2},{4,5},{5,4},{6,7},{7,6},{8,9},{9,8},{10,11... | collective-permute-start | bytes 3145736 | tf_op jit(solution)/shard_map/ppermute | solution.py:82
  156.7 24.8 %collective-permute-start.22 = (bf16[256,2048]{1,0:T(8,128)(2,1)S(1)}, bf16[256,2048]{1,0:T(8,128)(2,1)S(1)}, u32[]{:S(2)}, u32[]{:S(2)}) collective-permute-start(bf16[256,2048]{1,0:T(8,128)(2,1)S(1)} %collective-permute-done.21), channel_id=1, source_target_pairs={{0,2},{2,6},{6,4},{4,0},{1,3},{3,7},{7,5},{5,1},{8,10},{10,14},{14... | collective-permute-start | bytes 3145736 | tf_op jit(solution)/shard_map/ppermute | solution.py:116
  156.7 49.3 %collective-permute-start.29 = (bf16[256,2048]{1,0:T(8,128)(2,1)S(1)}, bf16[256,2048]{1,0:T(8,128)(2,1)S(1)}, u32[]{:S(2)}, u32[]{:S(2)}) collective-permute-start(bf16[256,2048]{1,0:T(8,128)(2,1)S(1)} %collective-permute-done.21), channel_id=1, source_target_pairs={{0,8},{8,0},{16,24},{24,16},{1,9},{9,1},{17,25},{25,17},{2,10},{10... | collective-permute-start | bytes 3145736 | tf_op jit(solution)/shard_map/ppermute | solution.py:119
  157.5 48.5 %collective-permute-start.6 = (bf16[512,768]{1,0:T(8,128)(2,1)S(1)}, bf16[512,768]{1,0:T(8,128)(2,1)S(1)}, u32[]{:S(2)}, u32[]{:S(2)}) collective-permute-start(bf16[512,768]{1,0:T(8,128)(2,1)S(1)} %copy-done.7), channel_id=1, source_target_pairs={{0,18},{1,22},{2,16},{3,20},{4,19},{5,23},{6,17},{7,21},{8,26},{9,... | collective-permute-start | bytes 2359304 | tf_op jit(solution)/shard_map/ppermute | solution.py:112
  161.6 44.6 %collective-permute-start.5 = (bf16[512,768]{1,0:T(8,128)(2,1)S(1)}, bf16[512,768]{1,0:T(8,128)(2,1)S(1)}, u32[]{:S(2)}, u32[]{:S(2)}) collective-permute-start(bf16[512,768]{1,0:T(8,128)(2,1)S(1)} %collective-permute-done.4), channel_id=1, source_target_pairs={{0,1},{1,0},{2,3},{3,2},{4,5},{5,4},{6,7},{7,6},{8,9},{9,8},{10,11... | collective-permute-start | bytes 2359304 | tf_op jit(solution)/shard_map/ppermute | solution.py:154
  181.4 84.9 %collective-permute-start.23 = (bf16[256,2048]{1,0:T(8,128)(2,1)S(1)}, bf16[256,2048]{1,0:T(8,128)(2,1)}, u32[]{:S(2)}, u32[]{:S(2)}) collective-permute-start(bf16[256,2048]{1,0:T(8,128)(2,1)S(1)} %convolution_convert_fusion), channel_id=1, source_target_pairs={{0,2},{2,6},{6,4},{4,0},{1,3},{3,7},{7,5},{5,1},{8,10},{10,14},{14... | collective-permute-start | bytes 3145736 | tf_op jit(solution)/shard_map/ppermute | solution.py:137
  189.4 30.2 %collective-permute-start.30 = (bf16[256,2048]{1,0:T(8,128)(2,1)S(1)}, bf16[256,2048]{1,0:T(8,128)(2,1)S(1)}, u32[]{:S(2)}, u32[]{:S(2)}) collective-permute-start(bf16[256,2048]{1,0:T(8,128)(2,1)S(1)} %collective-permute-done.22), channel_id=1, source_target_pairs={{0,8},{8,0},{16,24},{24,16},{1,9},{9,1},{17,25},{25,17},{2,10},{10... | collective-permute-start | bytes 3145736 | tf_op jit(solution)/shard_map/ppermute | solution.py:119
  213.9 58.0 %collective-permute-start.13 = (bf16[256,2048]{1,0:T(8,128)(2,1)}, bf16[256,2048]{1,0:T(8,128)(2,1)}, u32[]{:S(2)}, u32[]{:S(2)}) collective-permute-start(bf16[256,2048]{1,0:T(8,128)(2,1)} %convolution_convert_fusion.3), channel_id=1, source_target_pairs={{0,8},{8,0},{16,24},{24,16},{1,9},{9,1},{17,25},{25,17},{2,10},{10... | collective-permute-start | bytes 3145736 | tf_op jit(solution)/shard_map/ppermute | solution.py:161
  214.7 47.2 %collective-permute-start.15 = (bf16[256,2048]{1,0:T(8,128)(2,1)}, bf16[256,2048]{1,0:T(8,128)(2,1)}, u32[]{:S(2)}, u32[]{:S(2)}) collective-permute-start(bf16[256,2048]{1,0:T(8,128)(2,1)} %convolution_convert_fusion.1), channel_id=1, source_target_pairs={{0,8},{8,0},{16,24},{24,16},{1,9},{9,1},{17,25},{25,17},{2,10},{10... | collective-permute-start | bytes 3145736 | tf_op jit(solution)/shard_map/ppermute | solution.py:161
  227.0 46.8 %collective-permute-start.33 = (bf16[2048,256]{1,0:T(8,128)(2,1)}, bf16[2048,256]{1,0:T(8,128)(2,1)}, u32[]{:S(2)}, u32[]{:S(2)}) collective-permute-start(bf16[2048,256]{1,0:T(8,128)(2,1)} %convolution_convert_fusion.5), channel_id=1, source_target_pairs={{0,16},{8,24},{16,0},{24,8},{1,17},{9,25},{17,1},{25,9},{2,18},{10... | collective-permute-start | bytes 3145736 | tf_op jit(solution)/shard_map/ppermute | solution.py:181
  265.9 27.3 %collective-permute-start.17 = (bf16[256,2048]{1,0:T(8,128)(2,1)}, bf16[256,2048]{1,0:T(8,128)(2,1)}, u32[]{:S(2)}, u32[]{:S(2)}) collective-permute-start(bf16[256,2048]{1,0:T(8,128)(2,1)} %fusion.6), channel_id=1, source_target_pairs={{0,2},{2,6},{6,4},{4,0},{1,3},{3,7},{7,5},{5,1},{8,10},{10,14},{14... | collective-permute-start | bytes 3145736 | tf_op jit(solution)/shard_map/ppermute | solution.py:169
  270.1 43.9 %collective-permute-start.24 = (bf16[256,2048]{1,0:T(8,128)(2,1)}, bf16[256,2048]{1,0:T(8,128)(2,1)}, u32[]{:S(2)}, u32[]{:S(2)}) collective-permute-start(bf16[256,2048]{1,0:T(8,128)(2,1)} %fusion.8), channel_id=1, source_target_pairs={{0,2},{2,6},{6,4},{4,0},{1,3},{3,7},{7,5},{5,1},{8,10},{10,14},{14... | collective-permute-start | bytes 3145736 | tf_op jit(solution)/shard_map/ppermute | solution.py:137
  271.7 46.1 %collective-permute-start.32 = (bf16[2048,256]{1,0:T(8,128)(2,1)}, bf16[2048,256]{1,0:T(8,128)(2,1)}, u32[]{:S(2)}, u32[]{:S(2)}) collective-permute-start(bf16[2048,256]{1,0:T(8,128)(2,1)} %convolution_convert_fusion.6), channel_id=1, source_target_pairs={{0,16},{8,24},{16,0},{24,8},{1,17},{9,25},{17,1},{25,9},{2,18},{10... | collective-permute-start | bytes 3145736 | tf_op jit(solution)/shard_map/ppermute | solution.py:181
  271.9 89.3 %collective-permute-start.31 = (bf16[2048,256]{1,0:T(8,128)(2,1)S(1)}, bf16[2048,256]{1,0:T(8,128)(2,1)}, u32[]{:S(2)}, u32[]{:S(2)}) collective-permute-start(bf16[2048,256]{1,0:T(8,128)(2,1)S(1)} %convolution_convert_fusion.7), channel_id=1, source_target_pairs={{0,16},{8,24},{16,0},{24,8},{1,17},{9,25},{17,1},{25,9},{2,18},{10... | collective-permute-start | bytes 3145736 | tf_op jit(solution)/shard_map/ppermute | solution.py:181
  273.8 96.8 %collective-permute-start.14 = (bf16[256,2048]{1,0:T(8,128)(2,1)S(1)}, bf16[256,2048]{1,0:T(8,128)(2,1)}, u32[]{:S(2)}, u32[]{:S(2)}) collective-permute-start(bf16[256,2048]{1,0:T(8,128)(2,1)S(1)} %convolution_convert_fusion.4), channel_id=1, source_target_pairs={{0,8},{8,0},{16,24},{24,16},{1,9},{9,1},{17,25},{25,17},{2,10},{10... | collective-permute-start | bytes 3145736 | tf_op jit(solution)/shard_map/ppermute | solution.py:161
  293.3 32.2 %collective-permute-start.16 = (bf16[256,2048]{1,0:T(8,128)(2,1)S(1)}, bf16[256,2048]{1,0:T(8,128)(2,1)}, u32[]{:S(2)}, u32[]{:S(2)}) collective-permute-start(bf16[256,2048]{1,0:T(8,128)(2,1)S(1)} %convolution_convert_fusion.2), channel_id=1, source_target_pairs={{0,8},{8,0},{16,24},{24,16},{1,9},{9,1},{17,25},{25,17},{2,10},{10... | collective-permute-start | bytes 3145736 | tf_op jit(solution)/shard_map/ppermute | solution.py:161
  314.0 27.3 %collective-permute-start.18 = (bf16[256,2048]{1,0:T(8,128)(2,1)}, bf16[256,2048]{1,0:T(8,128)(2,1)}, u32[]{:S(2)}, u32[]{:S(2)}) collective-permute-start(bf16[256,2048]{1,0:T(8,128)(2,1)} %fusion.5), channel_id=1, source_target_pairs={{0,2},{2,6},{6,4},{4,0},{1,3},{3,7},{7,5},{5,1},{8,10},{10,14},{14... | collective-permute-start | bytes 3145736 | tf_op jit(solution)/shard_map/ppermute | solution.py:169
  317.8 43.3 %collective-permute-start.25 = (bf16[256,2048]{1,0:T(8,128)(2,1)}, bf16[256,2048]{1,0:T(8,128)(2,1)}, u32[]{:S(2)}, u32[]{:S(2)}) collective-permute-start(bf16[256,2048]{1,0:T(8,128)(2,1)} %fusion.7), channel_id=1, source_target_pairs={{0,2},{2,6},{6,4},{4,0},{1,3},{3,7},{7,5},{5,1},{8,10},{10,14},{14... | collective-permute-start | bytes 3145736 | tf_op jit(solution)/shard_map/ppermute | solution.py:137
  361.1 23.5 %collective-permute-start.26 = (bf16[256,2048]{1,0:T(8,128)(2,1)S(1)}, bf16[256,2048]{1,0:T(8,128)(2,1)}, u32[]{:S(2)}, u32[]{:S(2)}) collective-permute-start(bf16[256,2048]{1,0:T(8,128)(2,1)S(1)} %fusion.4), channel_id=1, source_target_pairs={{0,2},{2,6},{6,4},{4,0},{1,3},{3,7},{7,5},{5,1},{8,10},{10,14},{14... | collective-permute-start | bytes 3145736 | tf_op jit(solution)/shard_map/ppermute | solution.py:169
  (15 other events, 473.7 us)

commit v3 on v2

v3 whole, which is shorter than its diff:
```python
import jax
import jax.numpy as jnp
from jax import lax
from jax.sharding import PartitionSpec as P

BF16 = jnp.bfloat16
F32 = jnp.float32


def ring_place(j, n):
    return jnp.where(j % 2 == 1, (j + 1) // 2, (n - j // 2) % n)


def ring_pairs(n):
    order = [0] + list(range(1, n, 2)) + list(range(n - 2, 0, -2))
    return [(order[p], order[(p + 1) % n]) for p in range(n)]


def dot_rows(a, b):
    return lax.dot_general(a, b, (((0,), (0,)), ((), ())), preferred_element_type=F32)


def dot_cols(a, b):
    return lax.dot_general(a, b, (((1,), (1,)), ((), ())), preferred_element_type=F32)


def build(mesh):
    ni, nj, nk = mesh.shape["ia"], mesh.shape["ja"], mesh.shape["ka"]
    assert ni == 4 and nj >= 4 and nj % nk == 0
    per = nj // nk
    swap_x = [(i, i ^ 1) for i in range(ni)]
    swap_y = [(i, i ^ 2) for i in range(ni)]
    ring = ring_pairs(nj)
    core_ring = [(k, (k + 1) % nk) for k in range(nk)]

    def deal_pairs(step, dy):
        pairs = []
        for i in range(ni):
            for j in range(nj):
                for k in range(nk):
                    to_j, to_k = per * k + (j + step) % per, j // per
                    pairs.append(
                        ((i * nj + j) * nk + k, ((i ^ (2 * dy)) * nj + to_j) * nk + to_k)
                    )
        return pairs

    def local(
        inputs,
        attn_out,
        grad_out,
        grad_query,
        grad_key,
        grad_value,
        query_weight,
        key_weight,
        value_weight,
    ):
        i, j, k = lax.axis_index("ia"), lax.axis_index("ja"), lax.axis_index("ka")
        tok, width = inputs.shape[1], inputs.shape[2]
        feat = grad_query.shape[2] // per
        place = ring_place(j, nj)
        grads = (grad_query, grad_key, grad_value)

        live = {}

        def gate(**arrived):
            live.update(arrived)
            names = sorted(live)
            live.update(zip(names, lax.optimization_barrier(tuple(live[name] for name in names))))

        def along_x(value):
            return lax.ppermute(value, "ia", swap_x)

        def along_y(value):
            return lax.ppermute(value, "ia", swap_y)

        def along_z(value):
            return lax.ppermute(value, "ja", ring)

        def keep(name, value, *start):
            live[name] = lax.dynamic_update_slice(live[name], value, start)

        deals = [(step, dy) for dy in range(2) for step in range(per)]

        def deal_piece(step, dy):
            chunk = (j + step) % per
            return jnp.concatenate(
                [
                    jnp.concatenate(
                        [
                            lax.dynamic_slice(
                                grad, (i ^ (2 * dy) ^ dx, 0, chunk * feat), (1, tok, feat)
                            ).reshape(tok, feat)
                            for grad in grads
                        ],
                        axis=1,
                    )
                    for dx in range(2)
                ],
                axis=0,
            )

        def deal(index):
            return lax.ppermute(
                live.pop(f"piece{index}"), ("ia", "ja", "ka"), deal_pairs(*deals[index])
            )

        def share(index):
            step, dy = deals[index]
            piece = live.pop(f"dealt{index}")
            for hop in range(nk):
                source = per * ((k - hop) % nk) + (j % per - step) % per
                slot = (place - ring_place(source, nj)) % nj
                keep("g", piece[None], slot, 0, dy * 3 * feat)
                if hop < nk - 1:
                    piece = lax.ppermute(piece, "ka", core_ring)

        def dealt_in(step):
            if step == nj - 1:
                return range(min(step - 1, len(deals)), len(deals))
            return range(step - 1, min(step, len(deals)))

        live["came"] = rows = inputs.reshape(tok, width)
        live["go0"] = grad_out.reshape(tok, width)
        live["wk"], live["wv"] = key_weight, value_weight
        live["g"] = jnp.zeros((nj, 2 * tok, 6 * feat), BF16)
        live["x"] = jnp.zeros((nj * 2 * tok, width), BF16)
        live["w"] = jnp.zeros((width, 6 * feat), BF16)
        live["piece0"] = deal_piece(*deals[0])
        for step in range(1, nj):
            flying = {"came": along_z(live["came"]), "swapped": along_x(live["came"])}
            for index in dealt_in(step):
                flying[f"dealt{index}"] = deal(index)
            if step == 1:
                flying["go1"], flying["go2"] = along_x(live["go0"]), along_y(live["go0"])
                flying["w3"] = along_y(query_weight)
                for index in range(1, len(deals)):
                    live[f"piece{index}"] = deal_piece(*deals[index])
                parts = [
                    jnp.concatenate(
                        [
                            lax.dynamic_index_in_dim(attn_out, i ^ r, 0, keepdims=False)
                            for r in range(ni)
                        ],
                        axis=0,
                    )
                ]
                for _ in range(nk - 1):
                    parts.append(lax.ppermute(parts[-1], "ka", core_ring))
                live["attn"] = jnp.stack(parts)
            elif step == 2:
                flying["go3"] = along_y(live["go1"])
                flying["w4"] = along_y(live["wk"])
                for w, weight in enumerate((query_weight, live.pop("wk"), live["wv"])):
                    keep("w", weight, 0, w * feat)
                keep("w", live.pop("w3"), 0, 3 * feat)
            elif step == 3:
                flying["w5"] = along_y(live.pop("wv"))
                keep("w", live.pop("w4"), 0, 4 * feat)
                live["go"] = jnp.concatenate([live.pop(f"go{r}") for r in range(ni)], axis=0)
            keep("x", live.pop("came"), 2 * (step - 1) * tok, 0)
            if step > 1:
                keep("x", live.pop("swapped"), (2 * step - 3) * tok, 0)
                for index in dealt_in(step - 1):
                    share(index)
            gate(**flying)

        for index in dealt_in(nj - 1):
            share(index)
        keep("w", live.pop("w5"), 0, 5 * feat)

        def output_chunk(step):
            back = (place - step) % nj
            dest = jnp.where(
                back == 0, 0, jnp.where(back <= nj // 2, 2 * back - 1, 2 * (nj - back))
            )
            part = lax.dynamic_slice(
                live["attn"],
                ((k - dest // per) % nk, 0, (dest % per) * feat),
                (1, ni * tok, feat),
            )
            return dot_rows(part.reshape(ni * tok, feat), live["go"])

        def other_chunk(step):
            return dot_cols(live["g"][step % nj, tok:], live["w"]).astype(BF16)

        def own_chunk(step):
            return dot_cols(live["g"][step % nj, :tok], live["w"])

        def weight_term(w, count):
            part = live["g"][:, :, w * feat : (w + count) * feat]
            return dot_rows(live["x"], part.reshape(nj * 2 * tok, count * feat))

        flying = {"out": along_z(output_chunk(1).astype(BF16)), "other": along_x(other_chunk(1))}
        keep("x", live.pop("swapped"), (2 * nj - 3) * tok, 0)
        keep("x", live["came"], (2 * nj - 2) * tok, 0)
        live["own"] = own_chunk(1)
        live["part"] = output_chunk(2)
        live["send"] = other_chunk(2)
        gate(**flying)

        for step in range(1, nj):
            own = live.pop("own") + live.pop("other").astype(F32)
            if step > 1:
                own = own + live.pop("sum").astype(F32)
            total = live.pop("part") + live.pop("out").astype(F32)
            flying = {"sum": along_z(own.astype(BF16)), "other": along_x(live.pop("send"))}
            if step < nj - 1:
                flying["out"] = along_z(total.astype(BF16))
                live["part"] = output_chunk((step + 2) % nj)
                live["send"] = other_chunk(step + 2)
            else:
                output_weight_grad = total
            live["own"] = own_chunk(step + 1)
            if step == 1:
                flying["swapped"] = along_x(live.pop("came"))
            elif step == 2:
                keep("x", live.pop("swapped"), (2 * nj - 1) * tok, 0)
                flying["query"] = along_y(weight_term(3, 1).astype(BF16))
                flying["key"] = along_y(weight_term(4, 1).astype(BF16))
            elif step == 3:
                flying["value"] = along_y(weight_term(5, 1).astype(BF16))
                query_weight_grad = weight_term(0, 1) + live.pop("query").astype(F32)
                key_weight_grad = weight_term(1, 1) + live.pop("key").astype(F32)
            gate(**flying)
        grad_inputs = live["own"] + live["other"].astype(F32) + live["sum"].astype(F32)
        grad_inputs = grad_inputs.astype(BF16).reshape(inputs.shape)
        value_weight_grad = weight_term(2, 1) + live["value"].astype(F32)
        weight_grads = (query_weight_grad, key_weight_grad, value_weight_grad)
        return (grad_inputs, *weight_grads, output_weight_grad)

    return local


def solution(mesh):
    return jax.shard_map(
        build(mesh),
        mesh=mesh,
        in_specs=(
            P("ia", "ja", "ka"),
            P(None, "ja", ("ia", "ka")),
            P("ia", "ja", "ka"),
            P(None, "ja", ("ia", "ka")),
            P(None, "ja", ("ia", "ka")),
            P(None, "ja", ("ia", "ka")),
            P("ka", ("ia", "ja")),
            P("ka", ("ia", "ja")),
            P("ka", ("ia", "ja")),
        ),
        out_specs=(
            P("ia", "ja", "ka"),
            P("ka", ("ia", "ja")),
            P("ka", ("ia", "ja")),
            P("ka", ("ia", "ja")),
            P(("ia", "ja"), "ka"),
        ),
        check_vma=False,
    )
```

time: 395 us -> 354 us (0.90)
  waiting for transfers between devices: 229 us -> 192 us
  local copies, waits for them, and re-layouts: 22.1 us -> 44.2 us
  starting transfers between devices: 60.1 us -> 44.3 us
  matrix products: 66.5 us -> 51.5 us
    ppermute x34 -> x35, waiting for transfers between devices: 229 us -> 192 us  [the longest x9 91.6 us: along_z(): return lax.ppermute(value, 'ja', ring)]
    dynamic_update_slice x8 -> x22, local copies, waits for them, and re-layouts: 4.22 us -> 29.4 us  [keep(): live[name] = lax.dynamic_update_slice(live[name], value, start)]
    ppermute x34 -> x35, starting transfers between devices: 60.1 us -> 44.3 us  [the longest x9 13.4 us: along_z(): return lax.ppermute(value, 'ja', ring)]
    dot_general x10, matrix products: 41 us -> 26 us  [dot_rows(): lax.dot_general(a, b, (((0,), (0,)), ((), ())), preferred_element_type=F32)]
    unnamed x38 -> x56, local copies, waits for them, and re-layouts: 12.4 us -> 1.08 us
    slice x0 -> x3, local copies, waits for them, and re-layouts: none -> 5.16 us  [weight_term(): part = live['g'][:, :, w * feat:(w + count) * feat]]
  transfers between devices with their start and end apart: 34 -> 35, of which waited for: 12 -> 16; matrix products, arithmetic and copies ran while one was open for 24% -> 27% of each run, Pallas kernels for 0% -> 0%
where the time goes in v3:
time: 354 us; the launch traced here: 348 us
  waiting for transfers between devices  192 us (54%)
  matrix products  51.5 us (15%)
  starting transfers between devices  44.3 us (13%)
  local copies, waits for them, and re-layouts  44.2 us (12%)
  other arithmetic  13.8 us (4%)
    ppermute x9, waiting for transfers between devices, along_z(): return lax.ppermute(value, 'ja', ring)  91.6 us
    ppermute x4, waiting for transfers between devices, deal(): lax.ppermute(live.pop(f'piece{index}'), ('ia', 'ja', 'ka'), deal_pairs(*d...  66.2 us
    dynamic_update_slice x22, local copies, waits for them, and re-layouts, keep(): live[name] = lax.dynamic_update_slice(live[name], value, start)  29.4 us
    dot_general x10, matrix products, dot_rows(): lax.dot_general(a, b, (((0,), (0,)), ((), ())), preferred_element_type=F32)  26 us
    dot_general x8, matrix products, dot_cols(): lax.dot_general(a, b, (((1,), (1,)), ((), ())), preferred_element_type=F32)  25.5 us
    ppermute x8, waiting for transfers between devices, along_y(): return lax.ppermute(value, 'ia', swap_y)  25.1 us
    ppermute x9, starting transfers between devices, along_z(): return lax.ppermute(value, 'ja', ring)  13.4 us
    ppermute x9, starting transfers between devices, along_x(): return lax.ppermute(value, 'ia', swap_x)  11 us
  transfers between devices with their start and end apart: 35, of which 16 were waited for; matrix products, arithmetic and copies ran while one was open for 27% of the time, Pallas kernels for 0%

profile of v3, /device:TPU:0, one launch (start us, length us, event | category | flops | bytes accessed | tf_op | source)
XLA Modules:
  0.0 347.8 jit_solution(14893092988225002700)
XLA Ops:
  13.8 5.7 %dynamic_update_slice.66 = bf16[2048,2048]{1,0:T(8,128)(2,1)} pad(bf16[256,2048]{1,0:T(8,128)(2,1)} %bitcast.6, bf16[]{:T(256)} %constant.371.clone.1), padding=0_1792x0_0 | pad | bytes 9437186 | tf_op jit(solution)/shard_map/dynamic_update_slice | solution.py:81
  25.9 26.8 %collective-permute-done.1 = bf16[256,2048]{1,0:T(8,128)(2,1)} collective-permute-done((bf16[256,2048]{1,0:T(8,128)(2,1)}, bf16[256,2048]{1,0:T(8,128)(2,1)}, u32[]{:S(2)}, u32[]{:S(2)}) %collective-permute-start.1) | collective-permute-done | bytes 1048608 | tf_op jit(solution)/shard_map/ppermute | solution.py:78
  56.0 3.9 %collective-permute-start.9 = (bf16[512,768]{1,0:T(8,128)(2,1)S(1)}, bf16[512,768]{1,0:T(8,128)(2,1)S(1)}, u32[]{:S(2)}, u32[]{:S(2)}) collective-permute-start(bf16[512,768]{1,0:T(8,128)(2,1)S(1)} %copy-done.12), channel_id=1, source_target_pairs={{0,1},{1,0},{2,3},{3,2},{4,5},{5,4},{6,7},{7,6},{8,9},{9,8},{10,11... | collective-permute-start | bytes 2359304 | tf_op jit(solution)/shard_map/ppermute | solution.py:116
  68.5 3.1 collective-permute-start.8
  73.1 3.4 broadcast_in_dim.31
  78.8 22.7 %collective-permute-done.8 = bf16[512,768]{1,0:T(8,128)(2,1)} collective-permute-done((bf16[512,768]{1,0:T(8,128)(2,1)S(1)}, bf16[512,768]{1,0:T(8,128)(2,1)}, u32[]{:S(2)}, u32[]{:S(2)}) %collective-permute-start.8) | collective-permute-done | bytes 786464 | tf_op jit(solution)/shard_map/ppermute | solution.py:104
  101.5 8.5 %collective-permute-done.12 = bf16[2048,256]{1,0:T(8,128)(2,1)S(1)} collective-permute-done((bf16[2048,256]{1,0:T(8,128)(2,1)S(1)}, bf16[2048,256]{1,0:T(8,128)(2,1)S(1)}, u32[]{:S(2)}, u32[]{:S(2)}) %collective-permute-start.12) | collective-permute-done | bytes 1048608 | tf_op jit(solution)/shard_map/ppermute | solution.py:75
  111.0 3.6 %collective-permute-start.13 = (bf16[256,2048]{1,0:T(8,128)(2,1)}, bf16[256,2048]{1,0:T(8,128)(2,1)S(1)}, u32[]{:S(2)}, u32[]{:S(2)}) collective-permute-start(bf16[256,2048]{1,0:T(8,128)(2,1)} %collective-permute-done.7), channel_id=1, source_target_pairs={{0,2},{2,6},{6,4},{4,0},{1,3},{3,7},{7,5},{5,1},{8,10},{10,14},{14... | collective-permute-start | bytes 3145736 | tf_op jit(solution)/shard_map/ppermute | solution.py:78
  127.7 2.9 bitcast_dynamic-update-slice_fusion.4
  130.5 43.5 %collective-permute-done.14 = bf16[512,768]{1,0:T(8,128)(2,1)S(1)} collective-permute-done((bf16[512,768]{1,0:T(8,128)(2,1)}, bf16[512,768]{1,0:T(8,128)(2,1)S(1)}, u32[]{:S(2)}, u32[]{:S(2)}) %collective-permute-start.14) | collective-permute-done | bytes 786464 | tf_op jit(solution)/shard_map/ppermute | solution.py:104
  182.2 2.9 convolution_convert_fusion.4
  186.5 3.9 %convolution_convert_fusion.2 = bf16[256,2048]{1,0:T(8,128)(2,1)} fusion(bf16[2048,1536]{1,0:T(8,128)(2,1)S(1)} %constant_dynamic-update-slice_fusion.3, bf16[4,512,1536]{2,1,0:T(8,128)(2,1)} %bitcast_dynamic-update-slice_fusion), kind=kOutput, calls=%fused_computation.6 | convolution fusion | flops 1611137024 | bytes 8126464 | tf_op jit(solution)/shard_map/dot_general | solution.py:24
  190.4 2.9 fusion.1
  193.4 8.8 %collective-permute-done.22 = bf16[256,2048]{1,0:T(8,128)(2,1)S(1)} collective-permute-done((bf16[256,2048]{1,0:T(8,128)(2,1)S(1)}, bf16[256,2048]{1,0:T(8,128)(2,1)S(1)}, u32[]{:S(2)}, u32[]{:S(2)}) %collective-permute-start.22) | collective-permute-done | bytes 1048608 | tf_op jit(solution)/shard_map/ppermute | solution.py:78
  202.2 7.9 %collective-permute-done.21 = bf16[256,2048]{1,0:T(8,128)(2,1)S(1)} collective-permute-done((bf16[256,2048]{1,0:T(8,128)(2,1)S(1)}, bf16[256,2048]{1,0:T(8,128)(2,1)S(1)}, u32[]{:S(2)}, u32[]{:S(2)}) %collective-permute-start.21) | collective-permute-done | bytes 1048608 | tf_op jit(solution)/shard_map/ppermute | solution.py:72
  215.1 3.9 %convolution_convert_fusion.1 = bf16[256,2048]{1,0:T(8,128)(2,1)} fusion(bf16[2048,1536]{1,0:T(8,128)(2,1)S(1)} %constant_dynamic-update-slice_fusion.3, bf16[4,512,1536]{2,1,0:T(8,128)(2,1)} %bitcast_dynamic-update-slice_fusion), kind=kOutput, calls=%fused_computation.5 | convolution fusion | flops 1611137024 | bytes 8126464 | tf_op jit(solution)/shard_map/dot_general | solution.py:24
  220.4 2.9 fusion.8
  223.3 14.1 %collective-permute-done.25 = bf16[256,2048]{1,0:T(8,128)(2,1)S(1)} collective-permute-done((bf16[256,2048]{1,0:T(8,128)(2,1)S(1)}, bf16[256,2048]{1,0:T(8,128)(2,1)S(1)}, u32[]{:S(2)}, u32[]{:S(2)}) %collective-permute-start.25) | collective-permute-done | bytes 1048608 | tf_op jit(solution)/shard_map/ppermute | solution.py:78
  237.5 20.4 %collective-permute-done.24 = bf16[256,2048]{1,0:T(8,128)(2,1)S(1)} collective-permute-done((bf16[256,2048]{1,0:T(8,128)(2,1)S(1)}, bf16[256,2048]{1,0:T(8,128)(2,1)S(1)}, u32[]{:S(2)}, u32[]{:S(2)}) %collective-permute-start.24) | collective-permute-done | bytes 1048608 | tf_op jit(solution)/shard_map/ppermute | solution.py:78
  269.0 3.6 %convolution_convert_fusion.7 = bf16[2048,256]{1,0:T(8,128)(2,1)} fusion(bf16[2048,2048]{1,0:T(8,128)(2,1)S(1)} %constant_dynamic-update-slice_fusion, bf16[2048,256]{1,0:T(8,128)(2,1)S(1)} %bitcast.152), kind=kOutput, calls=%fused_computation.11 | convolution fusion | flops 2148007936 | bytes 10485760 | tf_op jit(solution)/shard_map/dot_general | solution.py:20
  274.4 2.9 convolution_convert_fusion
  278.6 2.9 fusion.5
  281.6 5.5 %collective-permute-done.31 = bf16[256,2048]{1,0:T(8,128)(2,1)S(1)} collective-permute-done((bf16[256,2048]{1,0:T(8,128)(2,1)S(1)}, bf16[256,2048]{1,0:T(8,128)(2,1)S(1)}, u32[]{:S(2)}, u32[]{:S(2)}) %collective-permute-start.31) | collective-permute-done | bytes 1048608 | tf_op jit(solution)/shard_map/ppermute | solution.py:78
  287.0 5.8 %collective-permute-done.30 = bf16[2048,256]{1,0:T(8,128)(2,1)S(1)} collective-permute-done((bf16[2048,256]{1,0:T(8,128)(2,1)S(1)}, bf16[2048,256]{1,0:T(8,128)(2,1)S(1)}, u32[]{:S(2)}, u32[]{:S(2)}) %collective-permute-start.30) | collective-permute-done | bytes 1048608 | tf_op jit(solution)/shard_map/ppermute | solution.py:75
  292.8 13.1 %collective-permute-done.29 = bf16[256,2048]{1,0:T(8,128)(2,1)S(1)} collective-permute-done((bf16[256,2048]{1,0:T(8,128)(2,1)S(1)}, bf16[256,2048]{1,0:T(8,128)(2,1)S(1)}, u32[]{:S(2)}, u32[]{:S(2)}) %collective-permute-start.29) | collective-permute-done | bytes 1048608 | tf_op jit(solution)/shard_map/ppermute | solution.py:78
  305.9 5.5 %collective-permute-done.27 = bf16[2048,256]{1,0:T(8,128)(2,1)S(1)} collective-permute-done((bf16[2048,256]{1,0:T(8,128)(2,1)}, bf16[2048,256]{1,0:T(8,128)(2,1)S(1)}, u32[]{:S(2)}, u32[]{:S(2)}) %collective-permute-start.27) | collective-permute-done | bytes 1048608 | tf_op jit(solution)/shard_map/ppermute | solution.py:75
  321.8 4.0 %convolution_add_fusion.1 = f32[2048,256]{1,0:T(8,128)} fusion(bf16[2048,2048]{1,0:T(8,128)(2,1)S(1)} %constant_dynamic-update-slice_fusion, bf16[2048,256]{1,0:T(8,128)(2,1)S(1)} %bitcast.151, bf16[2048,256]{1,0:T(8,128)(2,1)S(1)} %collective-permute-done.27), kind=kOutput, calls=%fused_computation.2 | convolution fusion | flops 2148532224 | bytes 12582912 | tf_op jit(solution)/shard_map/dot_general | solution.py:20
  325.8 2.9 fusion.2
  328.8 4.0 %convolution_add_fusion.2 = f32[2048,256]{1,0:T(8,128)} fusion(bf16[2048,2048]{1,0:T(8,128)(2,1)S(1)} %constant_dynamic-update-slice_fusion, bf16[2048,256]{1,0:T(8,128)(2,1)S(1)} %bitcast.150, bf16[2048,256]{1,0:T(8,128)(2,1)S(1)} %collective-permute-done.30), kind=kOutput, calls=%fused_computation.3 | convolution fusion | flops 2148532224 | bytes 12582912 | tf_op jit(solution)/shard_map/dot_general | solution.py:20
  332.8 4.7 %collective-permute-done.34 = bf16[2048,256]{1,0:T(8,128)(2,1)S(1)} collective-permute-done((bf16[2048,256]{1,0:T(8,128)(2,1)S(1)}, bf16[2048,256]{1,0:T(8,128)(2,1)S(1)}, u32[]{:S(2)}, u32[]{:S(2)}) %collective-permute-start.34) | collective-permute-done | bytes 1048608 | tf_op jit(solution)/shard_map/ppermute | solution.py:75
  337.5 3.0 collective-permute-done.33
  341.8 4.0 %convolution_add_fusion = f32[2048,256]{1,0:T(8,128)} fusion(bf16[2048,2048]{1,0:T(8,128)(2,1)S(1)} %constant_dynamic-update-slice_fusion, bf16[2048,256]{1,0:T(8,128)(2,1)S(1)} %bitcast.149, bf16[2048,256]{1,0:T(8,128)(2,1)S(1)} %collective-permute-done.34), kind=kOutput, calls=%fused_computation.1 | convolution fusion | flops 2148532224 | bytes 12582912 | tf_op jit(solution)/shard_map/dot_general | solution.py:20
  (158 shorter events, 92.1 us)
Async XLA Ops:
  2.1 11.1 %collective-permute-start = (bf16[1024,512]{1,0:T(8,128)(2,1)S(1)}, bf16[1024,512]{1,0:T(8,128)(2,1)}, u32[]{:S(2)}, u32[]{:S(2)}) collective-permute-start(bf16[1024,512]{1,0:T(8,128)(2,1)S(1)} %get-tuple-element.197), channel_id=1, source_target_pairs={{0,1},{1,0},{2,3},{3,2},{4,5},{5,4},{6,7},{7,6},{8,9},{9,8},{10,11... | collective-permute-start | bytes 3145736 | tf_op jit(solution)/shard_map/ppermute | solution.py:149
  6.9 45.8 %collective-permute-start.3 = (bf16[256,2048]{1,0:T(8,128)(2,1)}, bf16[256,2048]{1,0:T(8,128)(2,1)}, u32[]{:S(2)}, u32[]{:S(2)}) collective-permute-start(bf16[256,2048]{1,0:T(8,128)(2,1)} %bitcast.13), channel_id=1, source_target_pairs={{0,8},{8,0},{16,24},{24,16},{1,9},{9,1},{17,25},{25,17},{2,10},{10... | collective-permute-start | bytes 3145736 | tf_op jit(solution)/shard_map/ppermute | solution.py:72
  9.6 43.2 %collective-permute-start.4 = (bf16[256,2048]{1,0:T(8,128)(2,1)}, bf16[256,2048]{1,0:T(8,128)(2,1)}, u32[]{:S(2)}, u32[]{:S(2)}) collective-permute-start(bf16[256,2048]{1,0:T(8,128)(2,1)} %bitcast.13), channel_id=1, source_target_pairs={{0,16},{8,24},{16,0},{24,8},{1,17},{9,25},{17,1},{25,9},{2,18},{10... | collective-permute-start | bytes 3145736 | tf_op jit(solution)/shard_map/ppermute | solution.py:75
  11.1 41.7 %collective-permute-start.1 = (bf16[256,2048]{1,0:T(8,128)(2,1)}, bf16[256,2048]{1,0:T(8,128)(2,1)}, u32[]{:S(2)}, u32[]{:S(2)}) collective-permute-start(bf16[256,2048]{1,0:T(8,128)(2,1)} %bitcast.6), channel_id=1, source_target_pairs={{0,2},{2,6},{6,4},{4,0},{1,3},{3,7},{7,5},{5,1},{8,10},{10,14},{14... | collective-permute-start | bytes 3145736 | tf_op jit(solution)/shard_map/ppermute | solution.py:78
  12.7 40.1 %collective-permute-start.5 = (bf16[256,2048]{1,0:T(8,128)(2,1)}, bf16[256,2048]{1,0:T(8,128)(2,1)}, u32[]{:S(2)}, u32[]{:S(2)}) collective-permute-start(bf16[256,2048]{1,0:T(8,128)(2,1)} %bitcast.6), channel_id=1, source_target_pairs={{0,8},{8,0},{16,24},{24,16},{1,9},{9,1},{17,25},{25,17},{2,10},{10... | collective-permute-start | bytes 3145736 | tf_op jit(solution)/shard_map/ppermute | solution.py:72
  13.2 40.2 %collective-permute-start.6 = (bf16[2048,256]{1,0:T(8,128)(2,1)}, bf16[2048,256]{1,0:T(8,128)(2,1)}, u32[]{:S(2)}, u32[]{:S(2)}) collective-permute-start(bf16[2048,256]{1,0:T(8,128)(2,1)} %param.15), channel_id=1, source_target_pairs={{0,16},{8,24},{16,0},{24,8},{1,17},{9,25},{17,1},{25,9},{2,18},{10... | collective-permute-start | bytes 3145736 | tf_op jit(solution)/shard_map/ppermute | solution.py:75
  53.4 48.2 %collective-permute-start.11 = (bf16[256,2048]{1,0:T(8,128)(2,1)}, bf16[256,2048]{1,0:T(8,128)(2,1)S(1)}, u32[]{:S(2)}, u32[]{:S(2)}) collective-permute-start(bf16[256,2048]{1,0:T(8,128)(2,1)} %collective-permute-done.1), channel_id=1, source_target_pairs={{0,8},{8,0},{16,24},{24,16},{1,9},{9,1},{17,25},{25,17},{2,10},{10... | collective-permute-start | bytes 3145736 | tf_op jit(solution)/shard_map/ppermute | solution.py:72
  54.7 55.4 %collective-permute-start.7 = (bf16[256,2048]{1,0:T(8,128)(2,1)}, bf16[256,2048]{1,0:T(8,128)(2,1)}, u32[]{:S(2)}, u32[]{:S(2)}) collective-permute-start(bf16[256,2048]{1,0:T(8,128)(2,1)} %collective-permute-done.1), channel_id=1, source_target_pairs={{0,2},{2,6},{6,4},{4,0},{1,3},{3,7},{7,5},{5,1},{8,10},{10,14},{14... | collective-permute-start | bytes 3145736 | tf_op jit(solution)/shard_map/ppermute | solution.py:78
  56.0 12.5 %collective-permute-start.9 = (bf16[512,768]{1,0:T(8,128)(2,1)S(1)}, bf16[512,768]{1,0:T(8,128)(2,1)S(1)}, u32[]{:S(2)}, u32[]{:S(2)}) collective-permute-start(bf16[512,768]{1,0:T(8,128)(2,1)S(1)} %copy-done.12), channel_id=1, source_target_pairs={{0,1},{1,0},{2,3},{3,2},{4,5},{5,4},{6,7},{7,6},{8,9},{9,8},{10,11... | collective-permute-start | bytes 2359304 | tf_op jit(solution)/shard_map/ppermute | solution.py:116
  62.3 39.3 %collective-permute-start.10 = (bf16[256,2048]{1,0:T(8,128)(2,1)}, bf16[256,2048]{1,0:T(8,128)(2,1)S(1)}, u32[]{:S(2)}, u32[]{:S(2)}) collective-permute-start(bf16[256,2048]{1,0:T(8,128)(2,1)} %collective-permute-done.3), channel_id=1, source_target_pairs={{0,16},{8,24},{16,0},{24,8},{1,17},{9,25},{17,1},{25,9},{2,18},{10... | collective-permute-start | bytes 3145736 | tf_op jit(solution)/shard_map/ppermute | solution.py:75
  63.8 46.3 %collective-permute-start.12 = (bf16[2048,256]{1,0:T(8,128)(2,1)S(1)}, bf16[2048,256]{1,0:T(8,128)(2,1)S(1)}, u32[]{:S(2)}, u32[]{:S(2)}) collective-permute-start(bf16[2048,256]{1,0:T(8,128)(2,1)S(1)} %copy-done.2), channel_id=1, source_target_pairs={{0,16},{8,24},{16,0},{24,8},{1,17},{9,25},{17,1},{25,9},{2,18},{10... | collective-permute-start | bytes 3145736 | tf_op jit(solution)/shard_map/ppermute | solution.py:75
  68.5 33.0 %collective-permute-start.8 = (bf16[512,768]{1,0:T(8,128)(2,1)S(1)}, bf16[512,768]{1,0:T(8,128)(2,1)}, u32[]{:S(2)}, u32[]{:S(2)}) collective-permute-start(bf16[512,768]{1,0:T(8,128)(2,1)S(1)} %maximum_maximum_fusion.1), channel_id=1, source_target_pairs={{0,2},{1,6},{2,0},{3,4},{4,3},{5,7},{6,1},{7,5},{8,10},{9,14},{10,... | collective-permute-start | bytes 2359304 | tf_op jit(solution)/shard_map/ppermute | solution.py:104
  111.0 11.9 %collective-permute-start.16 = (bf16[512,768]{1,0:T(8,128)(2,1)}, bf16[512,768]{1,0:T(8,128)(2,1)}, u32[]{:S(2)}, u32[]{:S(2)}) collective-permute-start(bf16[512,768]{1,0:T(8,128)(2,1)} %collective-permute-done.8), channel_id=1, source_target_pairs={{0,1},{1,0},{2,3},{3,2},{4,5},{5,4},{6,7},{7,6},{8,9},{9,8},{10,11... | collective-permute-start | bytes 2359304 | tf_op jit(solution)/shard_map/ppermute | solution.py:116
  111.0 63.0 %collective-permute-start.13 = (bf16[256,2048]{1,0:T(8,128)(2,1)}, bf16[256,2048]{1,0:T(8,128)(2,1)S(1)}, u32[]{:S(2)}, u32[]{:S(2)}) collective-permute-start(bf16[256,2048]{1,0:T(8,128)(2,1)} %collective-permute-done.7), channel_id=1, source_target_pairs={{0,2},{2,6},{6,4},{4,0},{1,3},{3,7},{7,5},{5,1},{8,10},{10,14},{14... | collective-permute-start | bytes 3145736 | tf_op jit(solution)/shard_map/ppermute | solution.py:78
  114.7 59.4 %collective-permute-start.17 = (bf16[256,2048]{1,0:T(8,128)(2,1)}, bf16[256,2048]{1,0:T(8,128)(2,1)S(1)}, u32[]{:S(2)}, u32[]{:S(2)}) collective-permute-start(bf16[256,2048]{1,0:T(8,128)(2,1)} %collective-permute-done.7), channel_id=1, source_target_pairs={{0,8},{8,0},{16,24},{24,16},{1,9},{9,1},{17,25},{25,17},{2,10},{10... | collective-permute-start | bytes 3145736 | tf_op jit(solution)/shard_map/ppermute | solution.py:72
  115.4 58.7 %collective-permute-start.18 = (bf16[2048,256]{1,0:T(8,128)(2,1)S(1)}, bf16[2048,256]{1,0:T(8,128)(2,1)S(1)}, u32[]{:S(2)}, u32[]{:S(2)}) collective-permute-start(bf16[2048,256]{1,0:T(8,128)(2,1)S(1)} %copy-done.3), channel_id=1, source_target_pairs={{0,16},{8,24},{16,0},{24,8},{1,17},{9,25},{17,1},{25,9},{2,18},{10... | collective-permute-start | bytes 3145736 | tf_op jit(solution)/shard_map/ppermute | solution.py:75
  116.9 57.2 %collective-permute-start.14 = (bf16[512,768]{1,0:T(8,128)(2,1)}, bf16[512,768]{1,0:T(8,128)(2,1)S(1)}, u32[]{:S(2)}, u32[]{:S(2)}) collective-permute-start(bf16[512,768]{1,0:T(8,128)(2,1)} %maximum_maximum_fusion.2), channel_id=1, source_target_pairs={{0,16},{1,20},{2,18},{3,22},{4,17},{5,21},{6,19},{7,23},{8,24},{9,... | collective-permute-start | bytes 2359304 | tf_op jit(solution)/shard_map/ppermute | solution.py:104
  122.9 51.2 %collective-permute-start.15 = (bf16[512,768]{1,0:T(8,128)(2,1)S(1)}, bf16[512,768]{1,0:T(8,128)(2,1)S(1)}, u32[]{:S(2)}, u32[]{:S(2)}) collective-permute-start(bf16[512,768]{1,0:T(8,128)(2,1)S(1)} %copy-done.10), channel_id=1, source_target_pairs={{0,18},{1,22},{2,16},{3,20},{4,19},{5,23},{6,17},{7,21},{8,26},{9,... | collective-permute-start | bytes 2359304 | tf_op jit(solution)/shard_map/ppermute | solution.py:104
  175.9 26.3 %collective-permute-start.22 = (bf16[256,2048]{1,0:T(8,128)(2,1)S(1)}, bf16[256,2048]{1,0:T(8,128)(2,1)S(1)}, u32[]{:S(2)}, u32[]{:S(2)}) collective-permute-start(bf16[256,2048]{1,0:T(8,128)(2,1)S(1)} %convolution_convert_fusion.3), channel_id=1, source_target_pairs={{0,2},{2,6},{6,4},{4,0},{1,3},{3,7},{7,5},{5,1},{8,10},{10,14},{14... | collective-permute-start | bytes 3145736 | tf_op jit(solution)/shard_map/ppermute | solution.py:78
  185.2 24.9 %collective-permute-start.21 = (bf16[256,2048]{1,0:T(8,128)(2,1)S(1)}, bf16[256,2048]{1,0:T(8,128)(2,1)S(1)}, u32[]{:S(2)}, u32[]{:S(2)}) collective-permute-start(bf16[256,2048]{1,0:T(8,128)(2,1)S(1)} %convolution_convert_fusion.4), channel_id=1, source_target_pairs={{0,8},{8,0},{16,24},{24,16},{1,9},{9,1},{17,25},{25,17},{2,10},{10... | collective-permute-start | bytes 3145736 | tf_op jit(solution)/shard_map/ppermute | solution.py:72
  210.4 27.0 %collective-permute-start.25 = (bf16[256,2048]{1,0:T(8,128)(2,1)S(1)}, bf16[256,2048]{1,0:T(8,128)(2,1)S(1)}, u32[]{:S(2)}, u32[]{:S(2)}) collective-permute-start(bf16[256,2048]{1,0:T(8,128)(2,1)S(1)} %add_convert_fusion.4), channel_id=1, source_target_pairs={{0,2},{2,6},{6,4},{4,0},{1,3},{3,7},{7,5},{5,1},{8,10},{10,14},{14... | collective-permute-start | bytes 3145736 | tf_op jit(solution)/shard_map/ppermute | solution.py:78
  211.1 46.8 %collective-permute-start.24 = (bf16[256,2048]{1,0:T(8,128)(2,1)S(1)}, bf16[256,2048]{1,0:T(8,128)(2,1)S(1)}, u32[]{:S(2)}, u32[]{:S(2)}) collective-permute-start(bf16[256,2048]{1,0:T(8,128)(2,1)S(1)} %add_convert_fusion.5), channel_id=1, source_target_pairs={{0,2},{2,6},{6,4},{4,0},{1,3},{3,7},{7,5},{5,1},{8,10},{10,14},{14... | collective-permute-start | bytes 3145736 | tf_op jit(solution)/shard_map/ppermute | solution.py:78
  213.1 44.7 %collective-permute-start.23 = (bf16[256,2048]{1,0:T(8,128)(2,1)}, bf16[256,2048]{1,0:T(8,128)(2,1)S(1)}, u32[]{:S(2)}, u32[]{:S(2)}) collective-permute-start(bf16[256,2048]{1,0:T(8,128)(2,1)} %convolution_convert_fusion.2), channel_id=1, source_target_pairs={{0,8},{8,0},{16,24},{24,16},{1,9},{9,1},{17,25},{25,17},{2,10},{10... | collective-permute-start | bytes 3145736 | tf_op jit(solution)/shard_map/ppermute | solution.py:72
  214.0 45.2 %collective-permute-start.26 = (bf16[256,2048]{1,0:T(8,128)(2,1)S(1)}, bf16[256,2048]{1,0:T(8,128)(2,1)S(1)}, u32[]{:S(2)}, u32[]{:S(2)}) collective-permute-start(bf16[256,2048]{1,0:T(8,128)(2,1)S(1)} %collective-permute-done.13), channel_id=1, source_target_pairs={{0,8},{8,0},{16,24},{24,16},{1,9},{9,1},{17,25},{25,17},{2,10},{10... | collective-permute-start | bytes 3145736 | tf_op jit(solution)/shard_map/ppermute | solution.py:72
  259.8 27.3 %collective-permute-start.31 = (bf16[256,2048]{1,0:T(8,128)(2,1)S(1)}, bf16[256,2048]{1,0:T(8,128)(2,1)S(1)}, u32[]{:S(2)}, u32[]{:S(2)}) collective-permute-start(bf16[256,2048]{1,0:T(8,128)(2,1)S(1)} %add_convert_fusion.2), channel_id=1, source_target_pairs={{0,2},{2,6},{6,4},{4,0},{1,3},{3,7},{7,5},{5,1},{8,10},{10,14},{14... | collective-permute-start | bytes 3145736 | tf_op jit(solution)/shard_map/ppermute | solution.py:78
  266.6 26.2 %collective-permute-start.30 = (bf16[2048,256]{1,0:T(8,128)(2,1)S(1)}, bf16[2048,256]{1,0:T(8,128)(2,1)S(1)}, u32[]{:S(2)}, u32[]{:S(2)}) collective-permute-start(bf16[2048,256]{1,0:T(8,128)(2,1)S(1)} %convolution_convert_fusion.6), channel_id=1, source_target_pairs={{0,16},{8,24},{16,0},{24,8},{1,17},{9,25},{17,1},{25,9},{2,18},{10... | collective-permute-start | bytes 3145736 | tf_op jit(solution)/shard_map/ppermute | solution.py:75
  268.5 37.4 %collective-permute-start.29 = (bf16[256,2048]{1,0:T(8,128)(2,1)S(1)}, bf16[256,2048]{1,0:T(8,128)(2,1)S(1)}, u32[]{:S(2)}, u32[]{:S(2)}) collective-permute-start(bf16[256,2048]{1,0:T(8,128)(2,1)S(1)} %add_convert_fusion.3), channel_id=1, source_target_pairs={{0,2},{2,6},{6,4},{4,0},{1,3},{3,7},{7,5},{5,1},{8,10},{10,14},{14... | collective-permute-start | bytes 3145736 | tf_op jit(solution)/shard_map/ppermute | solution.py:78
  272.6 38.8 %collective-permute-start.27 = (bf16[2048,256]{1,0:T(8,128)(2,1)}, bf16[2048,256]{1,0:T(8,128)(2,1)S(1)}, u32[]{:S(2)}, u32[]{:S(2)}) collective-permute-start(bf16[2048,256]{1,0:T(8,128)(2,1)} %convolution_convert_fusion.7), channel_id=1, source_target_pairs={{0,16},{8,24},{16,0},{24,8},{1,17},{9,25},{17,1},{25,9},{2,18},{10... | collective-permute-start | bytes 3145736 | tf_op jit(solution)/shard_map/ppermute | solution.py:75
  273.1 38.3 %collective-permute-start.28 = (bf16[256,2048]{1,0:T(8,128)(2,1)S(1)}, bf16[256,2048]{1,0:T(8,128)(2,1)S(1)}, u32[]{:S(2)}, u32[]{:S(2)}) collective-permute-start(bf16[256,2048]{1,0:T(8,128)(2,1)S(1)} %copy-done.23), channel_id=1, source_target_pairs={{0,8},{8,0},{16,24},{24,16},{1,9},{9,1},{17,25},{25,17},{2,10},{10... | collective-permute-start | bytes 3145736 | tf_op jit(solution)/shard_map/ppermute | solution.py:72
  316.2 21.4 %collective-permute-start.34 = (bf16[2048,256]{1,0:T(8,128)(2,1)S(1)}, bf16[2048,256]{1,0:T(8,128)(2,1)S(1)}, u32[]{:S(2)}, u32[]{:S(2)}) collective-permute-start(bf16[2048,256]{1,0:T(8,128)(2,1)S(1)} %convolution_convert_fusion.5), channel_id=1, source_target_pairs={{0,16},{8,24},{16,0},{24,8},{1,17},{9,25},{17,1},{25,9},{2,18},{10... | collective-permute-start | bytes 3145736 | tf_op jit(solution)/shard_map/ppermute | solution.py:75
  318.3 22.2 %collective-permute-start.33 = (bf16[256,2048]{1,0:T(8,128)(2,1)S(1)}, bf16[256,2048]{1,0:T(8,128)(2,1)S(1)}, u32[]{:S(2)}, u32[]{:S(2)}) collective-permute-start(bf16[256,2048]{1,0:T(8,128)(2,1)S(1)} %add_convert_fusion.1), channel_id=1, source_target_pairs={{0,2},{2,6},{6,4},{4,0},{1,3},{3,7},{7,5},{5,1},{8,10},{10,14},{14... | collective-permute-start | bytes 3145736 | tf_op jit(solution)/shard_map/ppermute | solution.py:78
  319.0 21.5 %collective-permute-start.32 = (bf16[256,2048]{1,0:T(8,128)(2,1)S(1)}, bf16[256,2048]{1,0:T(8,128)(2,1)S(1)}, u32[]{:S(2)}, u32[]{:S(2)}) collective-permute-start(bf16[256,2048]{1,0:T(8,128)(2,1)S(1)} %convolution_convert_fusion), channel_id=1, source_target_pairs={{0,8},{8,0},{16,24},{24,16},{1,9},{9,1},{17,25},{25,17},{2,10},{10... | collective-permute-start | bytes 3145736 | tf_op jit(solution)/shard_map/ppermute | solution.py:72
  (31 other events, 458.1 us)
